TPU v7x, 256 devices: a whole 4x4x8 slice. The times are simulated.
256 devices in a mesh: dp: 4 (over x_lo, core), expert: 64 (over x_hi, y, z).
Axes of the slice: x: 4 (x_hi: 2, x_lo: 2; x = x_hi * 2 + x_lo), y: 4, z: 8, core: 2. Of those that a mesh axis runs over, the one named last changes fastest.
Arguments:
- out_grad: bfloat16 [32768, 2048], P(('dp', 'expert')), may hold values from -0.59765625 to 0.59765625
- expert_ids: int32 [32768, 2], P(('dp', 'expert')), may hold values from 0 to 63, all different within a row; in each aligned block of 128 rows (0 to 127, 128 to 255, ...) at most 9 rows name the same one
- keep: int32 [32768, 2], P(('dp', 'expert')), may hold values 0 or 1
- probs: bfloat16 [32768, 2], P(('dp', 'expert')), may hold values from 0.099609375 to 1
- gate_saved: bfloat16 [4, 64, 64, 9, 1408], P('dp', 'expert'), may hold values from -6 to 6
- up_saved: bfloat16 [4, 64, 64, 9, 1408], P('dp', 'expert'), may hold values from -6 to 6
- down_weight: bfloat16 [64, 1408, 2048], P('expert', 'dp'), may hold values from -0.15625 to 0.15625
Outputs:
- weight_grad: bfloat16 [64, 1408, 2048], P('expert', 'dp')
- gate_grad: bfloat16 [4, 64, 64, 9, 1408], P('dp', 'expert')
- up_grad: bfloat16 [4, 64, 64, 9, 1408], P('dp', 'expert')
- prob_grad: float32 [32768, 2], P(('dp', 'expert'))
Inputs may be any that keep to these rules, and one draw needn't show every extreme that they name: `expert_ids`: among the 128 rows of one device, no expert is named by more than 9 rows, a bound that some block reaches; a row names 2 different experts.
All inputs are finite; a program needn't handle non-finite values. No bound on the sum of `keep` on one device may be relied on, other than what follows from the above.
Results may differ from a plain program's by a relative error of at most 0.015.
Values may be sent and summed in bfloat16 or wider, within the bound.
No kernel may reach another device: no remote copies, remote signals or barrier semaphores. Data moves between devices by JAX's collectives and lax.ppermute only.
A program may use at most 128 MiB of HBM per device.

v0:
```python
import jax
import jax.numpy as jnp
from jax import lax
from jax.sharding import PartitionSpec as P


def silu_parts(gate):
    sig = jax.nn.sigmoid(gate)
    return (gate * sig, sig * (1.0 + gate * (1.0 - sig)))


def local(out_grad, expert_ids, keep, probs, gate_saved, up_saved, down_weight):
    groups = lax.axis_size("expert")
    tok_rows, top = expert_ids.shape
    cap = gate_saved.shape[3]
    width = out_grad.shape[1]
    hidden_width = gate_saved.shape[4]
    total = groups * cap
    flat_ids = expert_ids.reshape(-1)
    onehot = (flat_ids[:, None] == jnp.arange(groups, dtype=jnp.int32)[None, :]).astype(jnp.int32)
    before = jnp.cumsum(onehot, axis=0) - onehot
    slot = jnp.sum(before * onehot, axis=1)
    kept = keep.reshape(-1) == 1
    dest = jnp.where(kept, flat_ids * cap + slot, total)
    pair_rows = jnp.repeat(out_grad, top, axis=0)
    send_rows = jnp.zeros((total, width), jnp.bfloat16).at[dest].set(pair_rows, mode="drop")
    send_probs = jnp.zeros((total,), jnp.bfloat16).at[dest].set(probs.reshape(-1), mode="drop")
    recv_rows, recv_probs = (
        lax.all_to_all(
            send_rows.reshape(groups, cap, width), "expert", split_axis=0, concat_axis=0, tiled=True
        ),
        lax.all_to_all(
            send_probs.reshape(groups, cap), "expert", split_axis=0, concat_axis=0, tiled=True
        ),
    )
    grad_in = recv_rows.reshape(total, width)
    gate = gate_saved.reshape(total, hidden_width).astype(jnp.float32)
    up = up_saved.reshape(total, hidden_width).astype(jnp.float32)
    act, slope = silu_parts(gate)
    hidden = (act * up).astype(jnp.bfloat16)
    scaled = (
        recv_probs.reshape(total, 1).astype(jnp.float32) * grad_in.astype(jnp.float32)
    ).astype(jnp.bfloat16)
    block = lax.all_gather(down_weight, "dp", axis=1, tiled=True)[0]
    left = hidden
    outs = jnp.dot(left, block, preferred_element_type=jnp.float32)
    part = lax.dot_general(
        scaled, block, (((1,), (1,)), ((), ())), preferred_element_type=jnp.float32
    )
    hidden_grad = part
    outs, hidden_grad = (outs, hidden_grad)
    outs = outs.astype(jnp.bfloat16)
    gate_grad = (hidden_grad * up * slope).astype(jnp.bfloat16).reshape(gate_saved.shape)
    up_grad = (hidden_grad * act).astype(jnp.bfloat16).reshape(up_saved.shape)
    safe_dest = jnp.minimum(dest, total - 1)
    returned = lax.all_to_all(
        outs.reshape(groups, cap, width), "expert", split_axis=0, concat_axis=0, tiled=True
    )
    picked = returned.reshape(total, width)[safe_dest]
    value = jnp.einsum("rd,rd->r", pair_rows, picked, preferred_element_type=jnp.float32)
    prob_grad = jnp.where(kept, value, 0.0).reshape(tok_rows, top)
    left = hidden
    share = lax.psum_scatter(
        lax.dot_general(
            left, scaled, (((0,), (0,)), ((), ())), preferred_element_type=jnp.float32
        ).astype(jnp.bfloat16),
        "dp",
        scatter_dimension=0,
        tiled=True,
    )
    weight_grad = share.reshape(down_weight.shape)
    return (weight_grad, gate_grad, up_grad, prob_grad)


def solution(mesh):
    placed = (
        P(("dp", "expert"), None),
        P(("dp", "expert"), None),
        P(("dp", "expert"), None),
        P(("dp", "expert"), None),
        P("dp", "expert", None, None, None),
        P("dp", "expert", None, None, None),
        P("expert", "dp", None),
    )
    return jax.shard_map(
        local,
        mesh=mesh,
        in_specs=placed,
        out_specs=(
            P("expert", "dp", None),
            P("dp", "expert", None, None, None),
            P("dp", "expert", None, None, None),
            P(("dp", "expert"), None),
        ),
        check_vma=False,
    )
```

profile of v0, /device:TPU:1, one launch (start us, length us, event | category | flops | bytes accessed | tf_op | source)
XLA Modules:
  0.0 289.0 jit_solution(1013417120366392685)
XLA Ops:
  12.8 2.2 scatter_custom_fusion
  15.7 15.1 %all-to-all-start = ((bf16[64,1,9]{2,1,0:T(2,128)(2,1)}), bf16[64,1,9]{2,1,0:T(2,128)(2,1)S(1)}, u32[]{:S(2)}, u32[]{:S(2)}) async-start(bf16[64,1,9]{2,1,0:T(2,128)(2,1)} %all_to_all.16), calls=%async_computation | async-start | bytes 65536 | tf_op jit(solution)/shard_map/all_to_all | solution.py:32
  30.9 1.7 broadcast_in_dim.24
  33.0 2.9 %scatter_custom_fusion.1 = bf16[576,2048]{1,0:T(8,128)(2,1)S(1)} fusion(s32[256]{0:T(256)S(1)} %bitcast.41, bf16[256,2048]{1,0:T(8,128)(2,1)S(1)} %reshape.192, bf16[]{:T(256)} %constant.9.clone.1), kind=kCustom, calls=%fused_computation.16 | custom fusion | bytes 2359298 | tf_op jit(solution)/shard_map/scatter | solution.py:26
  36.0 2.9 reshape.162
  38.8 2.8 all-to-all-done
  41.6 10.0 %all-to-all-start.1 = ((bf16[64,9,2048]{2,1,0:T(8,128)(2,1)}), bf16[64,9,2048]{2,1,0:T(8,128)(2,1)}, u32[]{:S(2)}, u32[]{:S(2)}) async-start(bf16[64,9,2048]{2,1,0:T(8,128)(2,1)} %reshape.162), calls=%async_computation.1 | async-start | bytes 8388608 | tf_op jit(solution)/shard_map/all_to_all | solution.py:29
  53.9 2.1 convert_element_type.72
  56.0 88.2 %all-to-all-done.1 = bf16[64,9,2048]{2,1,0:T(8,128)(2,1)} async-done(((bf16[64,9,2048]{2,1,0:T(8,128)(2,1)}), bf16[64,9,2048]{2,1,0:T(8,128)(2,1)}, u32[]{:S(2)}, u32[]{:S(2)}) %all-to-all-start.1) | async-done | bytes 2359328 | tf_op jit(solution)/shard_map/all_to_all | solution.py:29
  144.2 5.0 %multiply_convert_fusion = bf16[64,9,2048]{2,1,0:T(8,128)(2,1)} fusion(bf16[64,9,2048]{2,1,0:T(8,128)(2,1)} %all-to-all-done.1, f32[64,9]{1,0:T(8,128)S(1)} %bitcast.37), kind=kLoop, calls=%fused_computation.3 | loop fusion | flops 3538944 | bytes 4720896 | tf_op jit(solution)/shard_map/convert_element_type | solution.py:43
  149.2 3.4 %convert_element_type.79 = bf16[576,2048]{1,0:T(8,128)(2,1)S(1)} reshape(bf16[64,9,2048]{2,1,0:T(8,128)(2,1)} %multiply_convert_fusion) | data formatting | bytes 4718592 | tf_op jit(solution)/shard_map/convert_element_type | solution.py:43
  152.6 8.8 %convolution_convert_fusion = bf16[1408,2048]{1,0:T(8,128)(2,1)} fusion(bf16[576,1408]{1,0:T(8,128)(2,1)} %convert_element_type.72, bf16[576,2048]{1,0:T(8,128)(2,1)S(1)} %convert_element_type.79), kind=kOutput, calls=%fused_computation.4 | convolution fusion | flops 3324772352 | bytes 9748480 | tf_op jit(solution)/shard_map/dot_general | solution.py:64
  161.5 7.0 %fusion.4 = bf16[576,2048]{1,0:T(8,128)(2,1)S(1)} fusion(bf16[576,1408]{1,0:T(8,128)(2,1)} %convert_element_type.72, bf16[1,1408,2048]{2,1,0:T(8,128)(2,1)} %all-gather.2.cloned.1.call-done), kind=kOutput, calls=%fused_computation.13 | convolution fusion | flops 3323068416 | bytes 9748480 | tf_op jit(solution)/shard_map/dot_general | solution.py:46
  168.4 2.8 reshape.166
  171.3 11.5 %all-to-all-start.2 = ((bf16[64,9,2048]{2,1,0:T(8,128)(2,1)}), bf16[64,9,2048]{2,1,0:T(8,128)(2,1)}, u32[]{:S(2)}, u32[]{:S(2)}) async-start(bf16[64,9,2048]{2,1,0:T(8,128)(2,1)} %reshape.166), calls=%async_computation.3 | async-start | bytes 8388608 | tf_op jit(solution)/shard_map/all_to_all | solution.py:56
  182.8 3.5 %copy.36 = f32[1,1,64,9,1408]{4,3,2,1,0:T(8,128)} copy(bf16[1,1,64,9,1408]{4,2,3,1,0:T(8,128)(2,1)S(1)} %copy-done.1) | data formatting | bytes 4866048 | tf_op jit(solution)/shard_map/convert_element_type | solution.py:38
  186.3 3.5 %copy.37 = f32[1,1,64,9,1408]{4,3,2,1,0:T(8,128)} copy(bf16[1,1,64,9,1408]{4,2,3,1,0:T(8,128)(2,1)S(1)} %copy-done.3) | data formatting | bytes 4866048 | tf_op jit(solution)/shard_map/convert_element_type | solution.py:37
  189.9 3.7 %reshape.170 = f32[576,1408]{1,0:T(8,128)S(1)} reshape(f32[1,1,64,9,1408]{4,3,2,1,0:T(8,128)} %copy.36) | data formatting | bytes 6488064 | tf_op jit(solution)/shard_map/convert_element_type | solution.py:38
  193.6 5.0 %reshape.171 = f32[576,1408]{1,0:T(8,128)} reshape(f32[1,1,64,9,1408]{4,3,2,1,0:T(8,128)} %copy.37) | data formatting | bytes 6488064 | tf_op jit(solution)/shard_map/convert_element_type | solution.py:37
  198.6 10.6 %multiply_convert_fusion.1 = (bf16[576,1408]{1,0:T(8,128)(2,1)}, bf16[576,1408]{1,0:T(8,128)(2,1)}) fusion(f32[576,1408]{1,0:T(8,128)} %reshape.171, f32[576,1408]{1,0:T(8,128)S(1)} %reshape.170, bf16[576,2048]{1,0:T(8,128)(2,1)} %copy-done.5, bf16[1,1408,2048]{2,1,0:T(8,128)(2,1)} %all-gather.2.cloned.1.call-done), kind=kOutput, calls=%fused_computation.9 | convolution fusion | flops 3332431872 | bytes 17858560 | tf_op jit(solution)/shard_map/dot_general | solution.py:47
  209.2 2.6 reshape.164
  213.3 2.6 reshape.165
  217.3 57.7 %all-to-all-done.2 = bf16[64,9,2048]{2,1,0:T(8,128)(2,1)} async-done(((bf16[64,9,2048]{2,1,0:T(8,128)(2,1)}), bf16[64,9,2048]{2,1,0:T(8,128)(2,1)}, u32[]{:S(2)}, u32[]{:S(2)}) %all-to-all-start.2) | async-done | bytes 2359328 | tf_op jit(solution)/shard_map/all_to_all | solution.py:56
  275.0 3.4 %reshape.167 = bf16[576,2048]{1,0:T(8,128)(2,1)S(1)} reshape(bf16[64,9,2048]{2,1,0:T(8,128)(2,1)} %all-to-all-done.2) | data formatting | bytes 4718592 | tf_op jit(solution)/shard_map/reshape | solution.py:59
  (50 shorter events, 16.0 us)
Async XLA Ops:
  7.2 154.3 %all-gather.2.cloned.1.call-start = ((), (), s32[]{:S(2)}) async-start(), calls=%async_computation.5 | async-start | bytes 7208960 | tf_op jit(solution)/shard_map/all_gather | solution.py:44
  15.7 25.9 %all-to-all-start = ((bf16[64,1,9]{2,1,0:T(2,128)(2,1)}), bf16[64,1,9]{2,1,0:T(2,128)(2,1)S(1)}, u32[]{:S(2)}, u32[]{:S(2)}) async-start(bf16[64,1,9]{2,1,0:T(2,128)(2,1)} %all_to_all.16), calls=%async_computation | async-start | bytes 65536 | tf_op jit(solution)/shard_map/all_to_all | solution.py:32
  33.0 2.9 %copy-start.4 = (bf16[256,2048]{1,0:T(8,128)(2,1)}, bf16[256,2048]{1,0:T(8,128)(2,1)S(1)}, u32[]{:S(2)}) copy-start(bf16[256,2048]{1,0:T(8,128)(2,1)S(1)} %reshape.192) | copy-start | bytes 3145732
  38.8 13.0 %copy-start = (bf16[1,1,64,9,1408]{4,2,3,1,0:T(8,128)(2,1)S(1)}, bf16[1,1,64,9,1408]{4,2,3,1,0:T(8,128)(2,1)}, u32[]{:S(2)}) copy-start(bf16[1,1,64,9,1408]{4,2,3,1,0:T(8,128)(2,1)} %param.12) | copy-start | bytes 4866052
  38.8 13.0 %copy-start.2 = (bf16[1,1,64,9,1408]{4,2,3,1,0:T(8,128)(2,1)S(1)}, bf16[1,1,64,9,1408]{4,2,3,1,0:T(8,128)(2,1)}, u32[]{:S(2)}) copy-start(bf16[1,1,64,9,1408]{4,2,3,1,0:T(8,128)(2,1)} %param.11) | copy-start | bytes 4866052
  41.6 102.6 %all-to-all-start.1 = ((bf16[64,9,2048]{2,1,0:T(8,128)(2,1)}), bf16[64,9,2048]{2,1,0:T(8,128)(2,1)}, u32[]{:S(2)}, u32[]{:S(2)}) async-start(bf16[64,9,2048]{2,1,0:T(8,128)(2,1)} %reshape.162), calls=%async_computation.1 | async-start | bytes 8388608 | tf_op jit(solution)/shard_map/all_to_all | solution.py:29
  51.6 230.5 %reduce-scatter.2.cloned.1.call-start = ((), (), s32[]{:S(2)}) async-start(), calls=%async_computation.4 | async-start | bytes 7208960 | tf_op jit(solution)/shard_map/reduce_scatter | solution.py:63
  152.6 8.9 %copy-start.5 = (bf16[576,2048]{1,0:T(8,128)(2,1)}, bf16[576,2048]{1,0:T(8,128)(2,1)S(1)}, u32[]{:S(2)}) copy-start(bf16[576,2048]{1,0:T(8,128)(2,1)S(1)} %convert_element_type.79) | copy-start | bytes 7077892
  171.3 11.5 %copy-start.1 = (bf16[1,1,64,9,1408]{4,2,3,1,0:T(8,128)(2,1)S(1)}, bf16[1,1,64,9,1408]{4,2,3,1,0:T(8,128)(2,1)}, u32[]{:S(2)}) copy-start(bf16[1,1,64,9,1408]{4,2,3,1,0:T(8,128)(2,1)} %param.12) | copy-start | bytes 4866052
  171.3 103.7 %all-to-all-start.2 = ((bf16[64,9,2048]{2,1,0:T(8,128)(2,1)}), bf16[64,9,2048]{2,1,0:T(8,128)(2,1)}, u32[]{:S(2)}, u32[]{:S(2)}) async-start(bf16[64,9,2048]{2,1,0:T(8,128)(2,1)} %reshape.166), calls=%async_computation.3 | async-start | bytes 8388608 | tf_op jit(solution)/shard_map/all_to_all | solution.py:56
  182.8 3.5 %copy-start.3 = (bf16[1,1,64,9,1408]{4,2,3,1,0:T(8,128)(2,1)S(1)}, bf16[1,1,64,9,1408]{4,2,3,1,0:T(8,128)(2,1)}, u32[]{:S(2)}) copy-start(bf16[1,1,64,9,1408]{4,2,3,1,0:T(8,128)(2,1)} %param.11) | copy-start | bytes 4866052
Sparse Core Ops, SparseCore 0:
  9.8 91.7 all-gather.1
  161.6 100.8 reduce-scatter.1
where the time goes:
time: 294 us; the launch traced here: 289 us
  waiting for transfers between devices  149 us (51%)
  local copies, waits for them, and re-layouts  52.2 us (18%)
  starting transfers between devices  36.9 us (13%)
  matrix products  26.4 us (9%)
  between operations  14.3 us (5%)
  other arithmetic  9.81 us (3%)
    all_to_all x1, waiting for transfers between devices, local(): lax.all_to_all(send_rows.reshape(groups, cap, width), 'expert', split_axi...  88.2 us
    all_to_all x1, waiting for transfers between devices, local(): lax.all_to_all(outs.reshape(groups, cap, width), 'expert', split_axis=0,...  57.7 us
    all_to_all x1, starting transfers between devices, local(): lax.all_to_all(send_probs.reshape(groups, cap), 'expert', split_axis=0, c...  15.1 us
    all_to_all x1, starting transfers between devices, local(): lax.all_to_all(outs.reshape(groups, cap, width), 'expert', split_axis=0,...  11.5 us
    dot_general x1, matrix products, local(): lax.dot_general(scaled, block, (((1,), (1,)), ((), ())), preferred_elemen...  10.6 us
    all_to_all x1, starting transfers between devices, local(): lax.all_to_all(send_rows.reshape(groups, cap, width), 'expert', split_axi...  10 us
    dot_general x1, matrix products, local(): lax.dot_general(left, scaled, (((0,), (0,)), ((), ())), preferred_element...  8.84 us
    convert_element_type x2, local copies, waits for them, and re-layouts, local(): gate = gate_saved.reshape(total, hidden_width).astype(jnp.float32)  8.46 us
  transfers between devices with their start and end apart: 5, of which 3 were waited for; matrix products, arithmetic and copies ran while one was open for 30% of the time, Pallas kernels for 0%

commit v1 on v0

v1 whole, which is shorter than its diff:
```python
import functools

import jax
import jax.numpy as jnp
from jax import lax
from jax.experimental import pallas as pl
from jax.experimental.pallas import tpu as pltpu
from jax.sharding import PartitionSpec as P

LANES = 128
BF16 = jnp.bfloat16
F32 = jnp.float32
MIB = 1 << 20


def pack_kernel(groups, cap, ids_ref, keep_ref, probs_ref, grad_ref, send_ref, dest_ref, wide):
    top, rows = ids_ref.shape
    blocks = grad_ref.shape[1] // LANES
    span = cap * blocks
    at_row = lax.broadcasted_iota(jnp.int32, (rows, rows), 0)
    at_col = lax.broadcasted_iota(jnp.int32, (rows, rows), 1)
    ids = [ids_ref[k : k + 1, :].astype(F32) for k in range(top)]
    columns = [
        jnp.sum(jnp.where(at_row == at_col, ids[k], 0.0), axis=1, keepdims=True) for k in range(top)
    ]
    dests = []
    for k in range(top):
        same = sum(jnp.where(columns[m] == ids[k], 1.0, 0.0) for m in range(top))
        slot = jnp.sum(jnp.where(at_row < at_col, same, 0.0), axis=0, keepdims=True).astype(jnp.int32)
        dest = slot * groups + ids_ref[k : k + 1, :]
        dest = jnp.where(keep_ref[k : k + 1, :] == 1, dest, -1)
        dest_ref[k : k + 1, :] = dest
        dests.append(dest)
    probs = [probs_ref[k : k + 1, :].astype(F32) for k in range(top)]
    for c in range(cap):
        row = lax.broadcasted_iota(jnp.int32, (groups, rows), 0) + c * groups
        pick = sum(jnp.where(row == dests[k], probs[k], 0.0) for k in range(top)).astype(BF16)
        out = jnp.dot(pick, grad_ref[...], preferred_element_type=F32)
        for j in range(blocks):
            wide[pl.ds(c * blocks + j, groups, stride=span), :] = out[:, j * LANES : (j + 1) * LANES]
    send_ref[...] = wide[...].astype(BF16)


def hidden_kernel(gate_ref, up_ref, me_ref, after_ref, far_other, far_mine, near_other, near_mine, whole):
    part = far_other.shape[0]
    step = 128
    for lo in range(0, gate_ref.shape[1], step):
        gate = gate_ref[:, lo : lo + step].astype(F32)
        hidden = gate * (1.0 / (1.0 + jnp.exp(-gate))) * up_ref[:, lo : lo + step].astype(F32)
        whole[lo : lo + step, :] = hidden.T.astype(BF16)
    me = me_ref[0]
    for flip, out in ((3, far_other), (2, far_mine), (1, near_other), (0, near_mine)):
        share = me ^ flip
        out[...] = whole[pl.ds(pl.multiple_of(share * part, 16), part), :]


def unpack_kernel(groups, cap, recv_ref, *refs):
    scaled_ref, wide = refs[-2:]
    blocks = scaled_ref.shape[1] // LANES
    span = cap * blocks
    wide[...] = recv_ref[...].astype(F32)
    for c in range(cap):
        for j in range(blocks):
            scaled_ref[c * groups : (c + 1) * groups, j * LANES : (j + 1) * LANES] = wide[
                pl.ds(c * blocks + j, groups, stride=span), :
            ].astype(BF16)


def finish_kernel(near_ref, *refs):
    out_ref = refs[-1]
    half = refs[0].shape[1]
    for k, far in enumerate(refs[:-1]):
        at = slice(k * half, (k + 1) * half)
        out_ref[:, at] = (near_ref[:, at] + far[...].astype(F32)).astype(BF16)


def grads_kernel(step, flips, scaled_ref, gate_ref, up_ref, *refs):
    shares, me_ref = refs[: len(flips)], refs[len(flips)]
    gate_grad_ref, up_grad_ref, score_ref, block_ref = refs[-4:]
    part = shares[0].shape[0]
    for flip, share in zip(flips, shares):
        block_ref[pl.ds(pl.multiple_of((me_ref[0] ^ flip) * part, 16), part), :] = share[...]
    width = block_ref.shape[0]
    total = jnp.zeros((scaled_ref.shape[0], 1), F32)
    for lo in range(0, width, step):
        hi = min(lo + step, width)
        hidden_grad = lax.dot_general(
            scaled_ref[...], block_ref[lo:hi, :], (((1,), (1,)), ((), ())), preferred_element_type=F32
        )
        gate = gate_ref[:, lo:hi].astype(F32)
        up = up_ref[:, lo:hi].astype(F32)
        sig = 1.0 / (1.0 + jnp.exp(-gate))
        act = gate * sig
        hidden = (act * up).astype(BF16).astype(F32)
        gate_grad_ref[:, lo:hi] = (hidden_grad * up * (sig * (1.0 + gate * (1.0 - sig)))).astype(BF16)
        up_grad_ref[:, lo:hi] = (hidden_grad * act).astype(BF16)
        total = total + jnp.sum(hidden * hidden_grad, axis=1, keepdims=True)
    score_ref[...] = total


def pick_kernel(back_ref, dest_ref, probs_ref, out_ref):
    total = back_ref.shape[0]
    top, rows = dest_ref.shape
    row = lax.broadcasted_iota(jnp.int32, (total, rows), 0)
    for k in range(top):
        dest = dest_ref[k : k + 1, :]
        value = jnp.sum(jnp.where(row == dest, back_ref[...], 0.0), axis=0, keepdims=True)
        out_ref[k : k + 1, :] = jnp.where(dest >= 0, value / probs_ref[k : k + 1, :].astype(F32), 0.0)


VMEM = pl.BlockSpec(memory_space=pltpu.VMEM)
SMEM = pl.BlockSpec(memory_space=pltpu.SMEM)
HELD = pl.BlockSpec(memory_space=pl.ANY)


def call(kernel, shapes, scratch, flops, moved, args, scalars=(), after=()):
    return pl.pallas_call(
        kernel,
        out_shape=[jax.ShapeDtypeStruct(s, t) for s, t in shapes],
        in_specs=[VMEM] * len(args) + [SMEM] * len(scalars) + [HELD] * len(after),
        out_specs=[VMEM] * len(shapes),
        scratch_shapes=scratch,
        compiler_params=pltpu.CompilerParams(vmem_limit_bytes=48 * MIB),
        cost_estimate=pl.CostEstimate(flops=flops, bytes_accessed=moved, transcendentals=0),
    )(*args, *scalars, *after)


def local(out_grad, expert_ids, keep, probs, gate_saved, up_saved, down_weight):
    groups = lax.axis_size("expert")
    replicas = lax.axis_size("dp")
    tok_rows, top = expert_ids.shape
    cap = gate_saved.shape[3]
    width = out_grad.shape[1]
    part = down_weight.shape[1]
    ff = gate_saved.shape[4]
    total = groups * cap
    blocks = width // LANES
    me = lax.axis_index("dp")
    here = me.astype(jnp.int32).reshape(1)
    over_core = [(r, r ^ 1) for r in range(replicas)]
    over_chip = [(r, r ^ 2) for r in range(replicas)]

    own = down_weight[0]
    beside = lax.ppermute(own, "dp", over_chip)

    ids, kept, prob = expert_ids.T, keep.T, probs.T
    send, dest = call(
        functools.partial(pack_kernel, groups, cap),
        [((total * blocks, LANES), BF16), ((top, tok_rows), jnp.int32)],
        [pltpu.VMEM((total * blocks, LANES), F32)],
        2 * total * tok_rows * width,
        6 * total * width,
        [ids, kept, prob, out_grad],
    )
    recv = lax.all_to_all(
        send.reshape(groups, cap * blocks, LANES), "expert", split_axis=0, concat_axis=0, tiled=True
    )

    gate = jnp.transpose(gate_saved[0, 0], (1, 0, 2)).reshape(total, ff)
    up = jnp.transpose(up_saved[0, 0], (1, 0, 2)).reshape(total, ff)
    pieces = call(
        hidden_kernel,
        [((part, total), BF16)] * 4,
        [pltpu.VMEM((ff, total), BF16)],
        20 * total * ff,
        20 * total * ff,
        [gate, up],
        [here],
        [dest],
    )
    far_other, far_mine, near_other, near_mine = pieces

    own, beside, _ = lax.optimization_barrier((own, beside, far_other))
    others = [lax.ppermute(own, "dp", over_core), lax.ppermute(beside, "dp", over_core)]

    (scaled,) = call(
        functools.partial(unpack_kernel, groups, cap),
        [((total, width), BF16)],
        [pltpu.VMEM((total * blocks, LANES), F32)],
        0,
        6 * total * width,
        [recv.reshape(total * blocks, LANES)],
        (),
        pieces,
    )

    def product(left, right):
        return jnp.dot(left, right, preferred_element_type=F32)

    halves = 2
    half = width // halves
    cols = [scaled[:, k * half : (k + 1) * half] for k in range(halves)]
    far = []
    for k in range(halves):
        got = lax.ppermute(product(far_other, cols[k]).astype(BF16), "dp", over_core)
        far.append((product(far_mine, cols[k]) + got.astype(F32)).astype(BF16))
    crossed = [lax.ppermute(f, "dp", over_chip) for f in far]
    got = lax.ppermute(product(near_other, scaled).astype(BF16), "dp", over_core)
    near = product(near_mine, scaled) + got.astype(F32)

    gate_grad, up_grad, score = call(
        functools.partial(grads_kernel, 256, (0, 2, 1, 3)),
        [((total, ff), BF16), ((total, ff), BF16), ((total, 1), F32)],
        [pltpu.VMEM((ff, width), BF16)],
        2 * total * width * ff,
        2 * (total * width + ff * width + 4 * total * ff),
        [scaled, gate, up, own, beside, *others],
        [here],
        far,
    )
    back = lax.all_to_all(
        score.reshape(cap, groups).T.reshape(groups, 1, cap), "expert", split_axis=0, concat_axis=0, tiled=True
    )
    (prob_grad,) = call(
        pick_kernel,
        [((top, tok_rows), F32)],
        [],
        total * tok_rows,
        total * LANES * 4,
        [back.reshape(groups, cap).T.reshape(total, 1), dest, prob],
    )
    (weight_grad,) = call(
        finish_kernel,
        [((part, width), BF16)],
        [],
        part * width,
        8 * part * width,
        [near, *crossed],
    )

    def bins(x):
        return jnp.transpose(x.reshape(cap, groups, ff), (1, 0, 2)).reshape(gate_saved.shape)

    return weight_grad[None], bins(gate_grad), bins(up_grad), prob_grad.T


def solution(mesh):
    placed = (
        P(("dp", "expert"), None),
        P(("dp", "expert"), None),
        P(("dp", "expert"), None),
        P(("dp", "expert"), None),
        P("dp", "expert", None, None, None),
        P("dp", "expert", None, None, None),
        P("expert", "dp", None),
    )
    return jax.shard_map(
        local,
        mesh=mesh,
        in_specs=placed,
        out_specs=(
            P("expert", "dp", None),
            P("dp", "expert", None, None, None),
            P("dp", "expert", None, None, None),
            P(("dp", "expert"), None),
        ),
        check_vma=False,
    )
```

time: 294 us -> 141 us (0.48); the launches traced: 289 us -> 141 us
  waiting for transfers between devices: 149 us -> 51.4 us
  local copies, waits for them, and re-layouts: 52.2 us -> 12.2 us
  blocking collectives: 0 us -> 22.9 us
  Pallas kernels: 0 us -> 22.5 us
  matrix products: 26.4 us -> 9.78 us
  starting transfers between devices: 36.9 us -> 21.1 us
  between operations: 14.3 us -> 0.78 us
  other arithmetic: 9.81 us -> 0.17 us
    all_to_all x3 -> x1, waiting for transfers between devices: 149 us -> 0.01 us  [local(): lax.all_to_all(send.reshape(groups, cap * blocks, LANES), 'expert', split...]
    ppermute x0 -> x8, waiting for transfers between devices: none -> 51.4 us  [the longest x1 51.4 us: local(): beside = lax.ppermute(own, 'dp', over_chip)]
    all_to_all x0 -> x1, blocking collectives: none -> 22.9 us  [local(): lax.all_to_all(score.reshape(cap, groups).T.reshape(groups, 1, cap), 'exp...]
    pallas_call x0 -> x6, Pallas kernels: none -> 22.5 us  [call(): pl.pallas_call(kernel, out_shape=[jax.ShapeDtypeStruct(s, t) for s, t in...]
    convert_element_type x7 -> x0, local copies, waits for them, and re-layouts: 22 us -> none  [the longest x2 8.46 us: local(): gate = gate_saved.reshape(total, hidden_width).astype(jnp.float32)]
    all_to_all x3 -> x1, starting transfers between devices: 36.6 us -> 15.6 us  [local(): lax.all_to_all(send.reshape(groups, cap * blocks, LANES), 'expert', split...]
    dot_general x3 -> x6, matrix products: 26.4 us -> 9.78 us  [product(): return jnp.dot(left, right, preferred_element_type=F32)]
    reshape x8 -> x3, local copies, waits for them, and re-layouts: 14.9 us -> 0.43 us  [the longest x1 0.26 us: local(): back.reshape(groups, cap).T.reshape(total, 1)]
  transfers between devices with their start and end apart: 5 -> 9, of which waited for: 3 -> 1; matrix products, arithmetic and copies ran while one was open for 30% -> 7% of each run, Pallas kernels for 0% -> 13%
where the time goes in v1:
time: 141 us
  waiting for transfers between devices  51.4 us (36%)
  blocking collectives  22.9 us (16%)
  Pallas kernels  22.5 us (16%)
  starting transfers between devices  21.1 us (15%)
  local copies, waits for them, and re-layouts  12.2 us (9%)
  matrix products  9.78 us (7%)
    ppermute x1, waiting for transfers between devices, local(): beside = lax.ppermute(own, 'dp', over_chip)  51.4 us
    all_to_all x1, blocking collectives, local(): lax.all_to_all(score.reshape(cap, groups).T.reshape(groups, 1, cap), 'exp...  22.9 us
    pallas_call x6, Pallas kernels, call(): pl.pallas_call(kernel, out_shape=[jax.ShapeDtypeStruct(s, t) for s, t in...  22.5 us
    all_to_all x1, starting transfers between devices, local(): lax.all_to_all(send.reshape(groups, cap * blocks, LANES), 'expert', split...  15.6 us
    unnamed x38, local copies, waits for them, and re-layouts  11.7 us
    dot_general x6, matrix products, product(): return jnp.dot(left, right, preferred_element_type=F32)  9.78 us
  transfers between devices with their start and end apart: 9, of which 1 were waited for; matrix products, arithmetic and copies ran while one was open for 7% of the time, Pallas kernels for 13%

profile of v1, /device:TPU:1, one launch (start us, length us, event | category | flops | bytes accessed | tf_op | source)
XLA Modules:
  0.0 140.8 jit_solution(13083489802809335497)
XLA Ops:
  1.3 1.0 copy-done.16
  3.7 2.1 %shard_map.102 = (bf16[9216,128]{1,0:T(8,128)(2,1)S(1)}, s32[2,128]{1,0:T(2,128)S(1)}) custom-call(s32[2,128]{1,0:T(2,128)S(1)} %bitcast.50, s32[2,128]{1,0:T(2,128)S(1)} %bitcast.51, bf16[2,128]{1,0:T(2,128)(2,1)S(1)} %bitcast.48, bf16[128,2048]{1,0:T(8,128)(2,1)S(1)} %copy-done.16), custom_call_target="tpu_custom_call" | custom-call | flops 301989888 | bytes 7077888 | tf_op jit(solution)/shard_map/pallas_call | solution.py:117
  5.8 1.5 %copy-done.4 = bf16[9216,128]{1,0:T(8,128)(2,1)} copy-done((bf16[9216,128]{1,0:T(8,128)(2,1)}, bf16[9216,128]{1,0:T(8,128)(2,1)S(1)}, u32[]{:S(2)}) %copy-start.4) | copy-done | bytes 2359320
  7.3 15.6 %all-to-all-start = ((bf16[64,144,128]{2,1,0:T(8,128)(2,1)}), bf16[64,144,128]{2,1,0:T(8,128)(2,1)}, u32[]{:S(2)}, u32[]{:S(2)}) async-start(bf16[64,144,128]{2,1,0:T(8,128)(2,1)} %bitcast.47), calls=%async_computation | async-start | bytes 4718592 | tf_op jit(solution)/shard_map/all_to_all | solution.py:155
  23.3 1.5 %shard_map.103 = (bf16[352,576]{1,0:T(8,128)(2,1)S(1)}, bf16[352,576]{1,0:T(8,128)(2,1)S(1)}, bf16[352,576]{1,0:T(8,128)(2,1)S(1)}, bf16[352,576]{1,0:T(8,128)(2,1)S(1)}) custom-call(bf16[576,1408]{1,0:T(8,128)(2,1)S(1)} %bitcast.44, bf16[576,1408]{1,0:T(8,128)(2,1)S(1)} %bitcast.46, s32[1]{0:T(128)} %bitcast.6.me_ref.refs_4_, ...), custom_call_target="tpu_custom_call" | custom-call | flops 16220160 | bytes 16220160 | tf_op jit(solution)/shard_map/pallas_call | solution.py:117
  24.8 0.8 copy-done.5
  26.3 0.8 copy-done.10
  27.8 51.4 %collective-permute-done.5.refs_1_ = bf16[352,2048]{1,0:T(8,128)(2,1)} collective-permute-done((bf16[352,2048]{1,0:T(8,128)(2,1)}, bf16[352,2048]{1,0:T(8,128)(2,1)}, u32[]{:S(2)}, u32[]{:S(2)}) %collective-permute-start.5) | collective-permute-done | bytes 1441824 | tf_op jit(solution)/shard_map/ppermute | solution.py:144
  79.2 1.6 %collective-permute-start.6 = (bf16[352,2048]{1,0:T(8,128)(2,1)}, bf16[352,2048]{1,0:T(8,128)(2,1)}, u32[]{:S(2)}, u32[]{:S(2)}) collective-permute-start(bf16[352,2048]{1,0:T(8,128)(2,1)} %bitcast.17.refs_0_), channel_id=1, source_target_pairs={{0,64},{64,0},{128,192},{192,128},{1,65},{65,1},{129,193},{193,129... | collective-permute-start | bytes 4325384 | tf_op jit(solution)/shard_map/ppermute | solution.py:174
  80.8 1.0 copy-done.6
  81.8 1.0 copy-done.9
  82.8 1.0 copy-done.11
  83.9 1.0 copy-done.13
  84.9 3.5 %shard_map.104.scaled_ref = bf16[576,2048]{1,0:T(8,128)(2,1)S(1)} custom-call(bf16[9216,128]{1,0:T(8,128)(2,1)} %bitcast.11.recv_ref, bf16[352,576]{1,0:T(8,128)(2,1)S(1)} %copy-done.11, bf16[352,576]{1,0:T(8,128)(2,1)S(1)} %copy-done.9, bf16[352,576]{1,0:T(8,128)(2,1)S(1)} %copy-done.13, bf16[352,576]{1,0:T(8,128)(2,1)S(1)} %copy-done.6), custom_call_target="tpu_custom_call" | custom-call | bytes 7077888 | tf_op jit(solution)/shard_map/pallas_call | solution.py:117
  89.7 2.4 %convolution_convert_fusion = bf16[352,2048]{1,0:T(8,128)(2,1)} fusion(bf16[352,576]{1,0:T(8,128)(2,1)S(1)} %copy-done.13, bf16[576,2048]{1,0:T(8,128)(2,1)S(1)} %shard_map.104.scaled_ref), kind=kOutput, calls=%fused_computation.1 | convolution fusion | flops 831193088 | bytes 4206592 | tf_op jit(solution)/shard_map/dot_general | solution.py:188
  93.6 1.7 %add_convert_fusion.refs_6_ = bf16[352,1024]{1,0:T(8,128)(2,1)} fusion(bf16[352,1024]{1,0:T(8,128)(2,1)S(1)} %collective-permute-done.3, bf16[352,576]{1,0:T(8,128)(2,1)S(1)} %copy-done.9, bf16[576,2048]{1,0:T(8,128)(2,1)S(1)} %shard_map.104.scaled_ref), kind=kOutput, calls=%fused_computation.2 | convolution fusion | flops 416317440 | bytes 3072000 | tf_op jit(solution)/shard_map/dot_general | solution.py:188
  95.3 1.2 collective-permute-start.4
  96.5 1.6 %add_convert_fusion.1.refs_5_ = bf16[352,1024]{1,0:T(8,128)(2,1)} fusion(bf16[352,1024]{1,0:T(8,128)(2,1)S(1)} %collective-permute-done.1, bf16[352,576]{1,0:T(8,128)(2,1)S(1)} %copy-done.9, bf16[576,2048]{1,0:T(8,128)(2,1)S(1)} %shard_map.104.scaled_ref), kind=kOutput, calls=%fused_computation.3 | convolution fusion | flops 416317440 | bytes 3072000 | tf_op jit(solution)/shard_map/dot_general | solution.py:188
  98.1 1.0 collective-permute-start.2
  99.1 12.0 %shard_map.106 = (bf16[576,1408]{1,0:T(8,128)(2,1)}, bf16[576,1408]{1,0:T(8,128)(2,1)}, f32[576,1]{1,0:T(8,128)S(1)}) custom-call(bf16[576,2048]{1,0:T(8,128)(2,1)} %copy-done, bf16[576,1408]{1,0:T(8,128)(2,1)} %bitcast.43, bf16[576,1408]{1,0:T(8,128)(2,1)} %bitcast.45, bf16[352,2048]{1,0:T(8,128)(2,1)} %bitcast.17.refs_0_, ...), custom_call_target="tpu_custom_call" | custom-call | flops 3321888768 | bytes 14614528 | tf_op jit(solution)/shard_map/pallas_call | solution.py:117
  111.4 22.9 %all_to_all.10 = f32[64,1,9]{2,1,0:T(1,128)S(1)} all-to-all(f32[64,1,9]{2,1,0:T(1,128)S(1)} %copy.12), channel_id=1, replica_groups=mesh['dp'=4,'expert'=64] {'expert'}, dimensions={0} | all-to-all | bytes 4608 | tf_op jit(solution)/shard_map/all_to_all | solution.py:211
  134.7 0.8 shard_map.107
  135.5 2.6 %convert_add_fusion.near_ref = f32[352,2048]{1,0:T(8,128)S(1)} fusion(bf16[352,2048]{1,0:T(8,128)(2,1)} %collective-permute-done, bf16[352,576]{1,0:T(8,128)(2,1)S(1)} %copy-done.7, bf16[576,2048]{1,0:T(8,128)(2,1)S(1)} %copy-done.1), kind=kOutput, calls=%fused_computation | convolution fusion | flops 831913984 | bytes 7090176 | tf_op jit(solution)/shard_map/dot_general | solution.py:188
  138.2 2.7 %shard_map.105 = bf16[352,2048]{1,0:T(8,128)(2,1)} custom-call(f32[352,2048]{1,0:T(8,128)S(1)} %convert_add_fusion.near_ref, bf16[352,1024]{1,0:T(8,128)(2,1)} %collective-permute-done.2.refs_0_, bf16[352,1024]{1,0:T(8,128)(2,1)} %collective-permute-done.4.refs_1_), custom_call_target="tpu_custom_call" | custom-call | flops 720896 | bytes 5767168 | tf_op jit(solution)/shard_map/pallas_call | solution.py:117
  (50 shorter events, 7.5 us)
Async XLA Ops:
  1.3 1.0 copy-start.16
  5.8 1.5 %copy-start.4 = (bf16[9216,128]{1,0:T(8,128)(2,1)}, bf16[9216,128]{1,0:T(8,128)(2,1)S(1)}, u32[]{:S(2)}) copy-start(bf16[9216,128]{1,0:T(8,128)(2,1)S(1)} %get-tuple-element.17) | copy-start | bytes 7077892
  7.3 16.0 %copy-start.2 = (bf16[1,1,64,9,1408]{4,2,3,1,0:T(8,128)(2,1)S(1)}, bf16[1,1,64,9,1408]{4,2,3,1,0:T(8,128)(2,1)}, u32[]{:S(2)}) copy-start(bf16[1,1,64,9,1408]{4,2,3,1,0:T(8,128)(2,1)} %param.11) | copy-start | bytes 4866052
  7.3 16.0 %copy-start.3 = (bf16[1,1,64,9,1408]{4,2,3,1,0:T(8,128)(2,1)S(1)}, bf16[1,1,64,9,1408]{4,2,3,1,0:T(8,128)(2,1)}, u32[]{:S(2)}) copy-start(bf16[1,1,64,9,1408]{4,2,3,1,0:T(8,128)(2,1)} %param.12) | copy-start | bytes 4866052
  7.3 73.5 %all-to-all-start = ((bf16[64,144,128]{2,1,0:T(8,128)(2,1)}), bf16[64,144,128]{2,1,0:T(8,128)(2,1)}, u32[]{:S(2)}, u32[]{:S(2)}) async-start(bf16[64,144,128]{2,1,0:T(8,128)(2,1)} %bitcast.47), calls=%async_computation | async-start | bytes 4718592 | tf_op jit(solution)/shard_map/all_to_all | solution.py:155
  22.9 56.3 %collective-permute-start.5 = (bf16[352,2048]{1,0:T(8,128)(2,1)}, bf16[352,2048]{1,0:T(8,128)(2,1)}, u32[]{:S(2)}, u32[]{:S(2)}) collective-permute-start(bf16[352,2048]{1,0:T(8,128)(2,1)} %bitcast.17.refs_0_), channel_id=1, source_target_pairs={{0,128},{64,192},{128,0},{192,64},{1,129},{65,193},{129,1},{193,65... | collective-permute-start | bytes 4325384 | tf_op jit(solution)/shard_map/ppermute | solution.py:144
  24.8 0.8 copy-start.5
  25.5 0.8 copy-start.8
  26.3 0.8 copy-start.10
  79.2 19.9 %collective-permute-start.6 = (bf16[352,2048]{1,0:T(8,128)(2,1)}, bf16[352,2048]{1,0:T(8,128)(2,1)}, u32[]{:S(2)}, u32[]{:S(2)}) collective-permute-start(bf16[352,2048]{1,0:T(8,128)(2,1)} %bitcast.17.refs_0_), channel_id=1, source_target_pairs={{0,64},{64,0},{128,192},{192,128},{1,65},{65,1},{129,193},{193,129... | collective-permute-start | bytes 4325384 | tf_op jit(solution)/shard_map/ppermute | solution.py:174
  80.8 18.3 %collective-permute-start.7 = (bf16[352,2048]{1,0:T(8,128)(2,1)}, bf16[352,2048]{1,0:T(8,128)(2,1)}, u32[]{:S(2)}, u32[]{:S(2)}) collective-permute-start(bf16[352,2048]{1,0:T(8,128)(2,1)} %collective-permute-done.5.refs_1_), channel_id=1, source_target_pairs={{0,64},{64,0},{128,192},{192,128},{1,65},{65,1},{129,193},{193,129... | collective-permute-start | bytes 4325384 | tf_op jit(solution)/shard_map/ppermute | solution.py:174
  80.8 1.0 copy-start.6
  81.8 1.0 copy-start.9
  82.8 1.0 copy-start.11
  83.9 1.0 copy-start.13
  88.4 8.1 %copy-start = (bf16[576,2048]{1,0:T(8,128)(2,1)}, bf16[576,2048]{1,0:T(8,128)(2,1)S(1)}, u32[]{:S(2)}) copy-start(bf16[576,2048]{1,0:T(8,128)(2,1)S(1)} %shard_map.104.scaled_ref) | copy-start | bytes 7077892
  89.1 4.5 %collective-permute-start.3 = (bf16[352,1024]{1,0:T(8,128)(2,1)S(1)}, bf16[352,1024]{1,0:T(8,128)(2,1)S(1)}, u32[]{:S(2)}, u32[]{:S(2)}) collective-permute-start(bf16[352,1024]{1,0:T(8,128)(2,1)S(1)} %convolution_convert_fusion.1), channel_id=1, source_target_pairs={{0,64},{64,0},{128,192},{192,128},{1,65},{65,1},{129,193},{193,129... | collective-permute-start | bytes 2162696 | tf_op jit(solution)/shard_map/ppermute | solution.py:195
  92.1 43.4 %collective-permute-start = (bf16[352,2048]{1,0:T(8,128)(2,1)}, bf16[352,2048]{1,0:T(8,128)(2,1)}, u32[]{:S(2)}, u32[]{:S(2)}) collective-permute-start(bf16[352,2048]{1,0:T(8,128)(2,1)} %convolution_convert_fusion), channel_id=1, source_target_pairs={{0,64},{64,0},{128,192},{192,128},{1,65},{65,1},{129,193},{193,129... | collective-permute-start | bytes 4325384 | tf_op jit(solution)/shard_map/ppermute | solution.py:198
  92.8 3.6 %collective-permute-start.1 = (bf16[352,1024]{1,0:T(8,128)(2,1)S(1)}, bf16[352,1024]{1,0:T(8,128)(2,1)S(1)}, u32[]{:S(2)}, u32[]{:S(2)}) collective-permute-start(bf16[352,1024]{1,0:T(8,128)(2,1)S(1)} %convolution_convert_fusion.2), channel_id=1, source_target_pairs={{0,64},{64,0},{128,192},{192,128},{1,65},{65,1},{129,193},{193,129... | collective-permute-start | bytes 2162696 | tf_op jit(solution)/shard_map/ppermute | solution.py:195
  95.3 42.9 %collective-permute-start.4 = (bf16[352,1024]{1,0:T(8,128)(2,1)}, bf16[352,1024]{1,0:T(8,128)(2,1)}, u32[]{:S(2)}, u32[]{:S(2)}) collective-permute-start(bf16[352,1024]{1,0:T(8,128)(2,1)} %add_convert_fusion.refs_6_), channel_id=1, source_target_pairs={{0,128},{64,192},{128,0},{192,64},{1,129},{65,193},{129,1},{193,65... | collective-permute-start | bytes 2162696 | tf_op jit(solution)/shard_map/ppermute | solution.py:197
  98.1 36.6 %copy-start.15 = (bf16[128,2]{0,1:T(2,128)(2,1)S(1)}, bf16[128,2]{0,1:T(2,128)(2,1)}, u32[]{:S(2)}) copy-start(bf16[128,2]{0,1:T(2,128)(2,1)} %param.10) | copy-start | bytes 1540
  98.1 37.4 %copy-start.1 = (bf16[576,2048]{1,0:T(8,128)(2,1)S(1)}, bf16[576,2048]{1,0:T(8,128)(2,1)}, u32[]{:S(2)}) copy-start(bf16[576,2048]{1,0:T(8,128)(2,1)} %copy-done) | copy-start | bytes 7077892
  98.1 37.4 %copy-start.7 = (bf16[352,576]{1,0:T(8,128)(2,1)S(1)}, bf16[352,576]{1,0:T(8,128)(2,1)}, u32[]{:S(2)}) copy-start(bf16[352,576]{1,0:T(8,128)(2,1)} %copy-done.5) | copy-start | bytes 1216516
  98.1 40.1 %collective-permute-start.2 = (bf16[352,1024]{1,0:T(8,128)(2,1)}, bf16[352,1024]{1,0:T(8,128)(2,1)}, u32[]{:S(2)}, u32[]{:S(2)}) collective-permute-start(bf16[352,1024]{1,0:T(8,128)(2,1)} %add_convert_fusion.1.refs_5_), channel_id=1, source_target_pairs={{0,128},{64,192},{128,0},{192,64},{1,129},{65,193},{129,1},{193,65... | collective-permute-start | bytes 2162696 | tf_op jit(solution)/shard_map/ppermute | solution.py:197
  (4 other events, 2.8 us)

commit v2 on v1

v2 whole, which is shorter than its diff:
```python
import functools

import jax
import jax.numpy as jnp
from jax import lax
from jax.experimental import pallas as pl
from jax.experimental.pallas import tpu as pltpu
from jax.sharding import PartitionSpec as P

LANES = 128
BF16 = jnp.bfloat16
F32 = jnp.float32
MIB = 1 << 20


def pack_kernel(groups, cap, ids_ref, keep_ref, probs_ref, grad_ref, send_ref, dest_ref, wide):
    top, rows = ids_ref.shape
    blocks = grad_ref.shape[1] // LANES
    span = cap * blocks
    turn = pl.program_id(0)

    @pl.when(turn == 0)
    def _():
        at_row = lax.broadcasted_iota(jnp.int32, (rows, rows), 0)
        at_col = lax.broadcasted_iota(jnp.int32, (rows, rows), 1)
        ids = [ids_ref[k : k + 1, :].astype(F32) for k in range(top)]
        columns = [
            jnp.sum(jnp.where(at_row == at_col, ids[k], 0.0), axis=1, keepdims=True) for k in range(top)
        ]
        for k in range(top):
            same = sum(jnp.where(columns[m] == ids[k], 1.0, 0.0) for m in range(top))
            slot = jnp.sum(jnp.where(at_row < at_col, same, 0.0), axis=0, keepdims=True).astype(jnp.int32)
            dest = slot * groups + ids_ref[k : k + 1, :]
            dest_ref[k : k + 1, :] = jnp.where(keep_ref[k : k + 1, :] == 1, dest, -1)

    some = send_ref.shape[0] // span
    expert = lax.broadcasted_iota(jnp.int32, (some, rows), 0) + turn * some
    probs = [probs_ref[k : k + 1, :].astype(F32) for k in range(top)]
    picks = [
        sum(jnp.where(expert + c * groups == dest_ref[k : k + 1, :], probs[k], 0.0) for k in range(top))
        for c in range(cap)
    ]
    out = jnp.dot(jnp.concatenate(picks, axis=0).astype(BF16), grad_ref[...], preferred_element_type=F32)
    for c in range(cap):
        for j in range(blocks):
            wide[pl.ds(c * blocks + j, some, stride=span), :] = out[
                c * some : (c + 1) * some, j * LANES : (j + 1) * LANES
            ]
    send_ref[...] = wide[...].astype(BF16)


def hidden_kernel(me_ref, gate_ref, up_ref, after_ref, *refs):
    pieces, token_ref, whole = refs[:-2], refs[-2], refs[-1]
    step = gate_ref.shape[1]
    turn = pl.program_id(0)
    gate = gate_ref[...].astype(F32)
    hidden = gate * (1.0 / (1.0 + jnp.exp(-gate))) * up_ref[...].astype(F32)
    whole[pl.ds(pl.multiple_of(turn * step, step), step), :] = hidden.T.astype(BF16)

    @pl.when(turn == pl.num_programs(0) - 1)
    def _():
        size = pieces[0].shape[0]
        cuts = len(pieces) // 4
        token_ref[...] = jnp.zeros_like(token_ref)
        for at, out in enumerate(pieces):
            flip, cut = 3 - at // cuts, at % cuts
            first = (me_ref[0] ^ flip) * (size * cuts) + cut * size
            out[...] = whole[pl.ds(pl.multiple_of(first, 16), size), :]


def unpack_kernel(groups, cap, recv_ref, *refs):
    cuts = (len(refs) - 7) // 2
    lefts, products = refs[:cuts], refs[cuts + 2 : 2 * cuts + 2]
    scaled_ref, wide, come, held, sems, left_sems = refs[cuts + 1], *refs[-5:]
    turns = come.shape[0]
    size = come.shape[1]
    loads = [
        pltpu.make_async_copy(recv_ref.at[pl.ds(i * size, size), :], come.at[i], sems.at[i])
        for i in range(turns)
    ]
    extra = [pltpu.make_async_copy(lefts[k], held.at[k], left_sems.at[k]) for k in range(cuts)]
    for load in loads + extra:
        load.start()
    blocks = scaled_ref.shape[1] // LANES
    span = cap * blocks
    for i in range(turns):
        loads[i].wait()
        wide[i * size : (i + 1) * size, :] = come[i].astype(F32)
    for c in range(cap):
        for j in range(blocks):
            scaled_ref[c * groups : (c + 1) * groups, j * LANES : (j + 1) * LANES] = wide[
                pl.ds(c * blocks + j, groups, stride=span), :
            ].astype(BF16)
    for k, out in enumerate(products):
        extra[k].wait()
        out[...] = jnp.dot(held[k], scaled_ref[...], preferred_element_type=F32).astype(BF16)


def grads_kernel(cap, step, flips, me_ref, scaled_ref, gate_ref, up_ref, *refs):
    gate_out, up_out, score_ref, token_ref, block_ref, gate_grad_ref, up_grad_ref, sems, out_sems = refs[-9:]
    stores = []
    shares = refs[: len(flips)]
    part = shares[0].shape[0]
    loads = []
    for at, flip in enumerate(flips):
        place = pl.ds(pl.multiple_of((me_ref[0] ^ flip) * part, 16), part)
        loads.append(pltpu.make_async_copy(shares[at], block_ref.at[place, :], sems.at[at]))
        loads[-1].start()
    for load in loads:
        load.wait()
    token_ref[...] = jnp.zeros_like(token_ref)
    width = block_ref.shape[0]
    total = 0.0
    for lo in range(0, width, step):
        hi = min(lo + step, width)
        hidden_grad = lax.dot_general(
            scaled_ref[...], block_ref[lo:hi, :], (((1,), (1,)), ((), ())), preferred_element_type=F32
        )
        for at in range(lo, hi, LANES):
            cols = slice(at, at + LANES)
            grad = hidden_grad[:, at - lo : at - lo + LANES]
            gate = gate_ref[:, cols].astype(F32)
            up = up_ref[:, cols].astype(F32)
            sig = 1.0 / (1.0 + jnp.exp(-gate))
            act = gate * sig
            up_grad = grad * act
            total = total + grad * (act * up).astype(BF16).astype(F32)
            gate_grad_ref[:, cols] = (grad * up * (sig * (1.0 + gate * (1.0 - sig)))).astype(BF16)
            up_grad_ref[:, cols] = up_grad.astype(BF16)
        here = (slice(None), pl.ds(lo, hi - lo))
        for side, (held, out) in enumerate(((gate_grad_ref, gate_out), (up_grad_ref, up_out))):
            stores.append(pltpu.make_async_copy(held.at[here], out.at[here], out_sems.at[side, lo // step]))
            stores[-1].start()
    scores = jnp.sum(total, axis=1, keepdims=True)
    groups = score_ref.shape[0]
    for c in range(cap):
        score_ref[:, c : c + 1] = scores[c * groups : (c + 1) * groups, :]
    for store in stores:
        store.wait()


def pick_kernel(back_ref, dest_ref, probs_ref, *refs):
    out_ref = refs[-1]
    groups, cap = back_ref.shape
    top, rows = dest_ref.shape
    row = lax.broadcasted_iota(jnp.int32, (groups, rows), 0)
    for k in range(top):
        dest = dest_ref[k : k + 1, :]
        value = jnp.zeros((groups, rows), F32)
        for c in range(cap):
            value = value + jnp.where(row + c * groups == dest, back_ref[:, c : c + 1], 0.0)
        value = jnp.sum(value, axis=0, keepdims=True)
        out_ref[k : k + 1, :] = jnp.where(dest >= 0, value / probs_ref[k : k + 1, :].astype(F32), 0.0)


def near_kernel(scaled_ref, *refs):
    cuts = (len(refs) - 2) // 2
    size = refs[0].shape[0]
    for k in range(cuts):
        total = jnp.dot(refs[k][...], scaled_ref[...], preferred_element_type=F32)
        refs[-1][k * size : (k + 1) * size, :] = total + refs[cuts + k][...].astype(F32)


def finish_kernel(near_ref, far_ref, *refs):
    refs[-1][...] = (near_ref[...] + far_ref[...].astype(F32)).astype(BF16)


SMEM = pl.BlockSpec(memory_space=pltpu.SMEM)
VMEM = pl.BlockSpec(memory_space=pltpu.VMEM)
HELD = pl.BlockSpec(memory_space=pl.ANY)
TOKEN = ((8, LANES), F32)


def fixed(shape):
    return pl.BlockSpec(shape, lambda i: (0,) * len(shape))


def rows_by(size, width):
    return pl.BlockSpec((size, width), lambda i: (i, 0))


def call(kernel, grid, args, outs, scratch, cost, after=(), aliases=None, limit=24):
    flops, moved = cost
    return pl.pallas_call(
        kernel,
        grid=() if grid is None else (grid,),
        out_shape=[jax.ShapeDtypeStruct(*o) for o, _ in outs],
        in_specs=[s for _, s in args] + [HELD] * len(after),
        out_specs=[s for _, s in outs],
        scratch_shapes=scratch,
        input_output_aliases=aliases or {},
        compiler_params=pltpu.CompilerParams(vmem_limit_bytes=limit * MIB),
        cost_estimate=pl.CostEstimate(flops=flops, bytes_accessed=moved, transcendentals=0),
    )(*[x for x, _ in args], *after)


def local(out_grad, expert_ids, keep, probs, gate_saved, up_saved, down_weight):
    groups = lax.axis_size("expert")
    replicas = lax.axis_size("dp")
    tok_rows, top = expert_ids.shape
    cap = gate_saved.shape[3]
    width = out_grad.shape[1]
    part = down_weight.shape[1]
    ff = gate_saved.shape[4]
    total = groups * cap
    blocks = width // LANES
    here = lax.axis_index("dp").astype(jnp.int32).reshape(1)
    over_core = [(r, r ^ 1) for r in range(replicas)]
    over_chip = [(r, r ^ 2) for r in range(replicas)]

    own = down_weight[0]
    beside = lax.ppermute(own, "dp", over_chip)
    own_there = lax.ppermute(own, "dp", over_core)

    ids, kept, prob = expert_ids.T, keep.T, probs.T
    small = fixed((top, tok_rows))
    turns = 4
    send, dest = call(
        functools.partial(pack_kernel, groups, cap),
        turns,
        [(ids, small), (kept, small), (prob, small), (out_grad, fixed((tok_rows, width)))],
        [
            (((total * blocks, LANES), BF16), rows_by(total * blocks // turns, LANES)),
            (((top, tok_rows), jnp.int32), small),
        ],
        [pltpu.VMEM((total * blocks // turns, LANES), F32)],
        (2 * total * tok_rows * width, 6 * total * width),
        limit=62,
    )
    recv = lax.all_to_all(
        send.reshape(groups, cap * blocks, LANES), "expert", split_axis=0, concat_axis=0, tiled=True
    )

    gate = jnp.transpose(gate_saved[0, 0], (1, 0, 2)).reshape(total, ff)
    up = jnp.transpose(up_saved[0, 0], (1, 0, 2)).reshape(total, ff)
    cuts = 2
    size = part // cuts
    by_lanes = pl.BlockSpec((total, LANES), lambda i: (0, i))
    *pieces, token = call(
        hidden_kernel,
        ff // LANES,
        [(here, SMEM), (gate, by_lanes), (up, by_lanes)],
        [(((size, total), BF16), fixed((size, total)))] * (4 * cuts)
        + [(TOKEN, fixed(TOKEN[0]))],
        [pltpu.VMEM((ff, total), BF16)],
        (20 * total * ff, 8 * total * ff),
        [dest],
    )
    far_other, far_mine, near_other, near_mine = [pieces[k * cuts : (k + 1) * cuts] for k in range(4)]

    left, half = fixed((size, total)), fixed((size, width))
    scaled, *first = call(
        functools.partial(unpack_kernel, groups, cap),
        None,
        [(recv.reshape(total * blocks, LANES), HELD)] + [(x, HELD) for x in far_other],
        [(((total, width), BF16), VMEM)] + [(((size, width), BF16), VMEM)] * cuts,
        [
            pltpu.VMEM((total * blocks, LANES), F32),
            pltpu.VMEM((turns, total * blocks // turns, LANES), BF16),
            pltpu.VMEM((cuts, size, total), BF16),
            pltpu.SemaphoreType.DMA((turns,)),
            pltpu.SemaphoreType.DMA((cuts,)),
        ],
        (2 * part * total * width, 8 * total * width),
        [token],
        limit=59,
    )

    def product(left):
        return jnp.dot(left, scaled, preferred_element_type=F32)

    def to_core(x):
        return lax.ppermute(x.astype(BF16), "dp", over_core)

    core_far = [to_core(x) for x in first]
    beside, first[0] = lax.optimization_barrier((beside, first[0]))
    others = [own_there, lax.ppermute(beside, "dp", over_core)]
    got = [to_core(product(x)) for x in near_other]
    far = [(product(x) + g.astype(F32)).astype(BF16) for x, g in zip(far_mine, core_far)]
    crossed = [lax.ppermute(x, "dp", over_chip) for x in far]

    gate_grad, up_grad, score, token = call(
        functools.partial(grads_kernel, cap, 2 * LANES, (0, 2, 1, 3)),
        None,
        [(here, SMEM)] + [(x, VMEM) for x in (scaled, gate, up)] + [(w, HELD) for w in (own, beside, *others)],
        [(((total, ff), BF16), HELD)] * 2 + [(((groups, cap), F32), VMEM), (TOKEN, VMEM)],
        [
            pltpu.VMEM((ff, width), BF16),
            pltpu.VMEM((total, ff), BF16),
            pltpu.VMEM((total, ff), BF16),
            pltpu.SemaphoreType.DMA((replicas,)),
            pltpu.SemaphoreType.DMA((2, -(-ff // (2 * LANES)))),
        ],
        (2 * total * width * ff, 2 * (total * width + ff * width + 4 * total * ff)),
        [far[-1]],
    )
    back = lax.all_to_all(
        score.reshape(groups, 1, cap), "expert", split_axis=0, concat_axis=0, tiled=True
    )
    (prob_grad,) = call(
        pick_kernel,
        1,
        [(back.reshape(groups, cap), fixed((groups, cap))), (dest, small), (prob, small)],
        [(((top, tok_rows), F32), small)],
        [],
        (total * tok_rows, total * LANES * 4),
        [token],
    )
    (near,) = call(
        near_kernel,
        1,
        [(scaled, fixed((total, width)))] + [(x, left) for x in near_mine] + [(x, half) for x in got],
        [(((part, width), F32), fixed((part, width)))],
        [],
        (2 * part * total * width, 8 * part * width),
        [token],
    )
    weight_grad = None
    for k in range(cuts):
        at = pl.BlockSpec((size, width), lambda i, k=k: (k, 0))
        (weight_grad,) = call(
            finish_kernel,
            1,
            [(near, at), (crossed[k], half)],
            [(((part, width), BF16), at)],
            [],
            (size * width, 8 * size * width),
            [] if k == 0 else [weight_grad],
            {} if k == 0 else {2: 0},
        )

    def bins(x):
        return jnp.transpose(x.reshape(cap, groups, ff), (1, 0, 2)).reshape(gate_saved.shape)

    return weight_grad[None], bins(gate_grad), bins(up_grad), prob_grad.T


def solution(mesh):
    placed = (
        P(("dp", "expert"), None),
        P(("dp", "expert"), None),
        P(("dp", "expert"), None),
        P(("dp", "expert"), None),
        P("dp", "expert", None, None, None),
        P("dp", "expert", None, None, None),
        P("expert", "dp", None),
    )
    return jax.shard_map(
        local,
        mesh=mesh,
        in_specs=placed,
        out_specs=(
            P("expert", "dp", None),
            P("dp", "expert", None, None, None),
            P("dp", "expert", None, None, None),
            P(("dp", "expert"), None),
        ),
        check_vma=False,
    )
```

time: 141 us -> 131 us (0.929)
  blocking collectives: 22.9 us -> 0 us
  starting transfers between devices: 21.1 us -> 30.9 us
  Pallas kernels: 22.5 us -> 29.3 us
  local copies, waits for them, and re-layouts: 12.2 us -> 6.14 us
  waiting for transfers between devices: 51.4 us -> 54.5 us
  matrix products: 9.78 us -> 8.23 us
    ppermute x1, waiting for transfers between devices: 51.4 us -> 0.01 us  [local(): beside = lax.ppermute(own, 'dp', over_chip)]
    all_to_all x1, waiting for transfers between devices: 0.01 us -> 44.4 us  [local(): lax.all_to_all(send.reshape(groups, cap * blocks, LANES), 'expert', split...]
    all_to_all x1 -> x0, blocking collectives: 22.9 us -> none  [local(): lax.all_to_all(score.reshape(cap, groups).T.reshape(groups, 1, cap), 'exp...]
    ppermute x7 -> x8, waiting for transfers between devices: 0.02 us -> 10.1 us  [the longest x2 10.1 us: local(): crossed = [lax.ppermute(x, 'dp', over_chip) for x in far]]
    all_to_all x0 -> x1, starting transfers between devices: none -> 7.48 us  [local(): lax.all_to_all(score.reshape(groups, 1, cap), 'expert', split_axis=0, con...]
    pallas_call x6 -> x8, Pallas kernels: 22.5 us -> 29.3 us  [call(): pl.pallas_call(kernel, grid=() if grid is None else (grid,), out_shape=[j...]
    unnamed x38 -> x44, local copies, waits for them, and re-layouts: 11.7 us -> 6.14 us
    ppermute x7 -> x8, starting transfers between devices: 5.14 us -> 7.43 us  [the longest x4 4.28 us: to_core(): return lax.ppermute(x.astype(BF16), 'dp', over_core)]
  transfers between devices with their start and end apart: 9 -> 11, of which waited for: 1 -> 2; matrix products, arithmetic and copies ran while one was open for 7% -> 6% of each run, Pallas kernels for 13% -> 18%
where the time goes in v2:
time: 131 us; the launch traced here: 130 us
  waiting for transfers between devices  54.5 us (42%)
  starting transfers between devices  30.9 us (24%)
  Pallas kernels  29.3 us (22%)
  matrix products  8.23 us (6%)
  local copies, waits for them, and re-layouts  6.14 us (5%)
    all_to_all x1, waiting for transfers between devices, local(): lax.all_to_all(send.reshape(groups, cap * blocks, LANES), 'expert', split...  44.4 us
    pallas_call x8, Pallas kernels, call(): pl.pallas_call(kernel, grid=() if grid is None else (grid,), out_shape=[j...  29.3 us
    all_to_all x1, starting transfers between devices, local(): lax.all_to_all(send.reshape(groups, cap * blocks, LANES), 'expert', split...  15.6 us
    ppermute x2, waiting for transfers between devices, local(): crossed = [lax.ppermute(x, 'dp', over_chip) for x in far]  10.1 us
    dot_general x4, matrix products, product(): return jnp.dot(left, scaled, preferred_element_type=F32)  8.23 us
    all_to_all x1, starting transfers between devices, local(): lax.all_to_all(score.reshape(groups, 1, cap), 'expert', split_axis=0, con...  7.48 us
    unnamed x44, local copies, waits for them, and re-layouts  6.14 us
    ppermute x4, starting transfers between devices, to_core(): return lax.ppermute(x.astype(BF16), 'dp', over_core)  4.28 us
  transfers between devices with their start and end apart: 11, of which 2 were waited for; matrix products, arithmetic and copies ran while one was open for 6% of the time, Pallas kernels for 18%

profile of v2, /device:TPU:1, one launch (start us, length us, event | category | flops | bytes accessed | tf_op | source)
XLA Modules:
  0.0 129.9 jit_solution(16122191440966932912)
XLA Ops:
  0.6 4.5 %shard_map.102 = (bf16[9216,128]{1,0:T(8,128)(2,1)}, s32[2,128]{1,0:T(2,128)}) custom-call(s32[2,128]{1,0:T(2,128)} %bitcast.54, s32[2,128]{1,0:T(2,128)} %bitcast.55, bf16[2,128]{1,0:T(2,128)(2,1)} %bitcast.46, bf16[128,2048]{1,0:T(8,128)(2,1)} %grad_ref.1), custom_call_target="tpu_custom_call" | custom-call | flops 301989888 | bytes 7077888 | tf_op jit(solution)/shard_map/pallas_call | solution.py:184
  5.2 15.6 %all-to-all-start = ((bf16[64,144,128]{2,1,0:T(8,128)(2,1)}), bf16[64,144,128]{2,1,0:T(8,128)(2,1)}, u32[]{:S(2)}, u32[]{:S(2)}) async-start(bf16[64,144,128]{2,1,0:T(8,128)(2,1)} %bitcast.52), calls=%async_computation | async-start | bytes 4718592 | tf_op jit(solution)/shard_map/all_to_all | solution.py:230
  21.2 1.2 collective-permute-start.3
  22.4 2.8 %shard_map.103 = (bf16[176,576]{1,0:T(8,128)(2,1)S(1)}, bf16[176,576]{1,0:T(8,128)(2,1)S(1)}, bf16[176,576]{1,0:T(8,128)(2,1)S(1)}, bf16[176,576]{1,0:T(8,128)(2...) custom-call(s32[1]{0:T(128)} %bitcast.5.me_ref, ...), custom_call_target="tpu_custom_call" | custom-call | flops 16220160 | bytes 6488064 | tf_op jit(solution)/shard_map/pallas_call | solution.py:184
  25.9 0.7 copy-done.7
  26.6 0.7 copy-done.9
  27.3 0.7 copy-done.11
  28.0 0.7 copy-done.13
  29.4 0.7 copy-done.20
  30.7 44.4 %all-to-all-done = bf16[64,144,128]{2,1,0:T(8,128)(2,1)} async-done(((bf16[64,144,128]{2,1,0:T(8,128)(2,1)}), bf16[64,144,128]{2,1,0:T(8,128)(2,1)}, u32[]{:S(2)}, u32[]{:S(2)}) %all-to-all-start) | async-done | bytes 2359328 | tf_op jit(solution)/shard_map/all_to_all | solution.py:230
  75.1 6.0 %shard_map.104 = (bf16[576,2048]{1,0:T(8,128)(2,1)}, bf16[176,2048]{1,0:T(8,128)(2,1)}, bf16[176,2048]{1,0:T(8,128)(2,1)}) custom-call(bf16[9216,128]{1,0:T(8,128)(2,1)} %bitcast.4.recv_ref, bf16[176,576]{1,0:T(8,128)(2,1)} %copy-done.19, bf16[176,576]{1,0:T(8,128)(2,1)} %copy-done.20, f32[8,128]{1,0:T(8,128)} %copy-done.21), custom_call_target="tpu_custom_call" | custom-call | flops 830472192 | bytes 9437184 | tf_op jit(solution)/shard_map/pallas_call | solution.py:184
  81.1 3.7 %collective-permute-start.7 = (bf16[176,2048]{1,0:T(8,128)(2,1)}, bf16[176,2048]{1,0:T(8,128)(2,1)S(1)}, u32[]{:S(2)}, u32[]{:S(2)}) collective-permute-start(bf16[176,2048]{1,0:T(8,128)(2,1)} %get-tuple-element.33), channel_id=1, source_target_pairs={{0,64},{64,0},{128,192},{192,128},{1,65},{65,1},{129,193},{193,129... | collective-permute-start | bytes 2162696 | tf_op jit(solution)/shard_map/ppermute | solution.py:273
  85.3 3.4 %convolution_convert_fusion = bf16[176,2048]{1,0:T(8,128)(2,1)} fusion(bf16[176,576]{1,0:T(8,128)(2,1)S(1)} %copy-done.10, bf16[576,2048]{1,0:T(8,128)(2,1)} %get-tuple-element.28.scaled_ref), kind=kOutput, calls=%fused_computation | convolution fusion | flops 415596544 | bytes 3282944 | tf_op jit(solution)/shard_map/dot_general | solution.py:270
  88.8 1.6 %convolution_convert_fusion.1 = bf16[176,2048]{1,0:T(8,128)(2,1)} fusion(bf16[176,576]{1,0:T(8,128)(2,1)S(1)} %copy-done.8, bf16[576,2048]{1,0:T(8,128)(2,1)S(1)} %copy-done), kind=kOutput, calls=%fused_computation.1 | convolution fusion | flops 415596544 | bytes 3282944 | tf_op jit(solution)/shard_map/dot_general | solution.py:270
  90.9 1.6 %add_convert_fusion = bf16[176,2048]{1,0:T(8,128)(2,1)} fusion(bf16[176,2048]{1,0:T(8,128)(2,1)S(1)} %collective-permute-done.7, bf16[176,576]{1,0:T(8,128)(2,1)S(1)} %copy-done.6, bf16[576,2048]{1,0:T(8,128)(2,1)S(1)} %copy-done), kind=kOutput, calls=%fused_computation.2 | convolution fusion | flops 416317440 | bytes 4003840 | tf_op jit(solution)/shard_map/dot_general | solution.py:270
  92.8 1.6 %add_convert_fusion.1.refs_4_ = bf16[176,2048]{1,0:T(8,128)(2,1)} fusion(bf16[176,2048]{1,0:T(8,128)(2,1)S(1)} %collective-permute-done.5, bf16[176,576]{1,0:T(8,128)(2,1)S(1)} %get-tuple-element.35, bf16[576,2048]{1,0:T(8,128)(2,1)S(1)} %copy-done), kind=kOutput, calls=%fused_computation.3 | convolution fusion | flops 416317440 | bytes 4003840 | tf_op jit(solution)/shard_map/dot_general | solution.py:270
  94.4 1.2 collective-permute-start.6
  95.6 8.7 %shard_map.105 = (bf16[576,1408]{1,0:T(8,128)(2,1)}, bf16[576,1408]{1,0:T(8,128)(2,1)}, f32[64,9]{1,0:T(8,128)S(1)}, f32[8,128]{1,0:T(8,128)S(1)}) custom-call(s32[1]{0:T(128)} %bitcast.5.me_ref, bf16[576,2048]{1,0:T(8,128)(2,1)S(1)} %copy-done, bf16[576,1408]{1,0:T(8,128)(2,1)S(1)} %bitcast.42, bf16[576,1408]{1,0:T(8,128)(2,1)S(1)} %bitcast.44, ...), custom_call_target="tpu_custom_call" | custom-call | flops 3321888768 | bytes 14614528 | tf_op jit(solution)/shard_map/pallas_call | solution.py:184
  104.9 7.5 %all-to-all-start.1 = ((f32[64,1,9]{2,1,0:T(1,128)}), f32[64,1,9]{2,1,0:T(1,128)}, u32[]{:S(2)}, u32[]{:S(2)}) async-start(f32[64,1,9]{2,1,0:T(1,128)} %bitcast.45), calls=%async_computation.1 | async-start | bytes 65536 | tf_op jit(solution)/shard_map/all_to_all | solution.py:297
  112.4 2.6 %shard_map.106.near_ref = f32[352,2048]{1,0:T(8,128)S(1)} custom-call(bf16[576,2048]{1,0:T(8,128)(2,1)S(1)} %copy-done, bf16[176,576]{1,0:T(8,128)(2,1)S(1)} %copy-done.12, bf16[176,576]{1,0:T(8,128)(2,1)S(1)} %copy-done.14, bf16[176,2048]{1,0:T(8,128)(2,1)} %collective-permute-done.refs_2_, bf16[176,2048]{1,0:T(8,128)(2,1)} %collective-permute-done.1.refs_3_, ...), custom_call_target="tpu_custom_call" | custom-call | flops 830472192 | bytes 5767168 | tf_op jit(solution)/shard_map/pallas_call | solution.py:184
  115.1 1.0 shard_map.107.refs_0_
  116.1 10.1 %collective-permute-done.6.far_ref = bf16[176,2048]{1,0:T(8,128)(2,1)} collective-permute-done((bf16[176,2048]{1,0:T(8,128)(2,1)}, bf16[176,2048]{1,0:T(8,128)(2,1)}, u32[]{:S(2)}, u32[]{:S(2)}) %collective-permute-start.6) | collective-permute-done | bytes 720928 | tf_op jit(solution)/shard_map/ppermute | solution.py:280
  126.2 2.1 %shard_map.108 = bf16[352,2048]{1,0:T(8,128)(2,1)} custom-call(f32[352,2048]{1,0:T(8,128)S(1)} %shard_map.106.near_ref, bf16[176,2048]{1,0:T(8,128)(2,1)} %collective-permute-done.6.far_ref, bf16[352,2048]{1,0:T(8,128)(2,1)} %shard_map.107.refs_0_), custom_call_target="tpu_custom_call", output_to_operand_aliasing={{}: (2, {})} | custom-call | flops 360448 | bytes 2883584 | tf_op jit(solution)/shard_map/pallas_call | solution.py:184
  128.3 1.6 %shard_map.109 = f32[2,128]{1,0:T(2,128)} custom-call(f32[64,9]{1,0:T(8,128)} %bitcast.26.back_ref, s32[2,128]{1,0:T(2,128)S(1)} %copy-done.16, bf16[2,128]{1,0:T(2,128)(2,1)S(1)} %bitcast.47, f32[8,128]{1,0:T(8,128)S(1)} %get-tuple-element.37.refs_4_.refs_0_), custom_call_target="tpu_custom_call" | custom-call | flops 73728 | bytes 294912 | tf_op jit(solution)/shard_map/pallas_call | solution.py:184
  (54 shorter events, 4.4 us)
Async XLA Ops:
  5.1 17.3 %copy-start.1 = (bf16[1,1,64,9,1408]{4,2,3,1,0:T(8,128)(2,1)S(1)}, bf16[1,1,64,9,1408]{4,2,3,1,0:T(8,128)(2,1)}, u32[]{:S(2)}) copy-start(bf16[1,1,64,9,1408]{4,2,3,1,0:T(8,128)(2,1)} %param.11) | copy-start | bytes 4866052
  5.1 17.3 %copy-start.3 = (bf16[1,1,64,9,1408]{4,2,3,1,0:T(8,128)(2,1)S(1)}, bf16[1,1,64,9,1408]{4,2,3,1,0:T(8,128)(2,1)}, u32[]{:S(2)}) copy-start(bf16[1,1,64,9,1408]{4,2,3,1,0:T(8,128)(2,1)} %param.12) | copy-start | bytes 4866052
  5.1 17.3 %copy-start.16 = (s32[2,128]{1,0:T(2,128)S(1)}, s32[2,128]{1,0:T(2,128)}, u32[]{:S(2)}) copy-start(s32[2,128]{1,0:T(2,128)} %get-tuple-element.24.after_ref.dest_ref) | copy-start | bytes 3076
  5.2 70.0 %all-to-all-start = ((bf16[64,144,128]{2,1,0:T(8,128)(2,1)}), bf16[64,144,128]{2,1,0:T(8,128)(2,1)}, u32[]{:S(2)}, u32[]{:S(2)}) async-start(bf16[64,144,128]{2,1,0:T(8,128)(2,1)} %bitcast.52), calls=%async_computation | async-start | bytes 4718592 | tf_op jit(solution)/shard_map/all_to_all | solution.py:230
  20.8 64.1 %collective-permute-start.2 = (bf16[352,2048]{1,0:T(8,128)(2,1)}, bf16[352,2048]{1,0:T(8,128)(2,1)}, u32[]{:S(2)}, u32[]{:S(2)}) collective-permute-start(bf16[352,2048]{1,0:T(8,128)(2,1)} %bitcast.48), channel_id=1, source_target_pairs={{0,128},{64,192},{128,0},{192,64},{1,129},{65,193},{129,1},{193,65... | collective-permute-start | bytes 4325384 | tf_op jit(solution)/shard_map/ppermute | solution.py:212
  21.2 73.2 %collective-permute-start.3 = (bf16[352,2048]{1,0:T(8,128)(2,1)}, bf16[352,2048]{1,0:T(8,128)(2,1)}, u32[]{:S(2)}, u32[]{:S(2)}) collective-permute-start(bf16[352,2048]{1,0:T(8,128)(2,1)} %bitcast.49), channel_id=1, source_target_pairs={{0,64},{64,0},{128,192},{192,128},{1,65},{65,1},{129,193},{193,129... | collective-permute-start | bytes 4325384 | tf_op jit(solution)/shard_map/ppermute | solution.py:213
  75.1 10.2 %copy-start.10 = (bf16[176,576]{1,0:T(8,128)(2,1)S(1)}, bf16[176,576]{1,0:T(8,128)(2,1)}, u32[]{:S(2)}) copy-start(bf16[176,576]{1,0:T(8,128)(2,1)} %copy-done.9) | copy-start | bytes 608260
  81.1 9.3 %collective-permute-start.7 = (bf16[176,2048]{1,0:T(8,128)(2,1)}, bf16[176,2048]{1,0:T(8,128)(2,1)S(1)}, u32[]{:S(2)}, u32[]{:S(2)}) collective-permute-start(bf16[176,2048]{1,0:T(8,128)(2,1)} %get-tuple-element.33), channel_id=1, source_target_pairs={{0,64},{64,0},{128,192},{192,128},{1,65},{65,1},{129,193},{193,129... | collective-permute-start | bytes 2162696 | tf_op jit(solution)/shard_map/ppermute | solution.py:273
  84.8 7.7 %collective-permute-start.5 = (bf16[176,2048]{1,0:T(8,128)(2,1)}, bf16[176,2048]{1,0:T(8,128)(2,1)S(1)}, u32[]{:S(2)}, u32[]{:S(2)}) collective-permute-start(bf16[176,2048]{1,0:T(8,128)(2,1)} %get-tuple-element.36), channel_id=1, source_target_pairs={{0,64},{64,0},{128,192},{192,128},{1,65},{65,1},{129,193},{193,129... | collective-permute-start | bytes 2162696 | tf_op jit(solution)/shard_map/ppermute | solution.py:273
  84.9 10.7 %collective-permute-start.4 = (bf16[352,2048]{1,0:T(8,128)(2,1)}, bf16[352,2048]{1,0:T(8,128)(2,1)S(1)}, u32[]{:S(2)}, u32[]{:S(2)}) collective-permute-start(bf16[352,2048]{1,0:T(8,128)(2,1)} %collective-permute-done.2.refs_1_), channel_id=1, source_target_pairs={{0,64},{64,0},{128,192},{192,128},{1,65},{65,1},{129,193},{193,129... | collective-permute-start | bytes 4325384 | tf_op jit(solution)/shard_map/ppermute | solution.py:277
  85.3 3.5 %copy-start = (bf16[576,2048]{1,0:T(8,128)(2,1)S(1)}, bf16[576,2048]{1,0:T(8,128)(2,1)}, u32[]{:S(2)}) copy-start(bf16[576,2048]{1,0:T(8,128)(2,1)} %get-tuple-element.28.scaled_ref) | copy-start | bytes 7077892
  85.3 3.5 %copy-start.8 = (bf16[176,576]{1,0:T(8,128)(2,1)S(1)}, bf16[176,576]{1,0:T(8,128)(2,1)}, u32[]{:S(2)}) copy-start(bf16[176,576]{1,0:T(8,128)(2,1)} %copy-done.7) | copy-start | bytes 608260
  88.7 23.7 %collective-permute-start.1 = (bf16[176,2048]{1,0:T(8,128)(2,1)}, bf16[176,2048]{1,0:T(8,128)(2,1)}, u32[]{:S(2)}, u32[]{:S(2)}) collective-permute-start(bf16[176,2048]{1,0:T(8,128)(2,1)} %convolution_convert_fusion), channel_id=1, source_target_pairs={{0,64},{64,0},{128,192},{192,128},{1,65},{65,1},{129,193},{193,129... | collective-permute-start | bytes 2162696 | tf_op jit(solution)/shard_map/ppermute | solution.py:273
  88.8 2.0 %copy-start.6 = (bf16[176,576]{1,0:T(8,128)(2,1)S(1)}, bf16[176,576]{1,0:T(8,128)(2,1)}, u32[]{:S(2)}) copy-start(bf16[176,576]{1,0:T(8,128)(2,1)} %copy-done.5) | copy-start | bytes 608260
  90.4 22.0 %collective-permute-start = (bf16[176,2048]{1,0:T(8,128)(2,1)}, bf16[176,2048]{1,0:T(8,128)(2,1)}, u32[]{:S(2)}, u32[]{:S(2)}) collective-permute-start(bf16[176,2048]{1,0:T(8,128)(2,1)} %convolution_convert_fusion.1), channel_id=1, source_target_pairs={{0,64},{64,0},{128,192},{192,128},{1,65},{65,1},{129,193},{193,129... | collective-permute-start | bytes 2162696 | tf_op jit(solution)/shard_map/ppermute | solution.py:273
  90.9 4.7 %copy-start.18 = (bf16[1,352,2048]{2,1,0:T(8,128)(2,1)S(1)}, bf16[1,352,2048]{2,1,0:T(8,128)(2,1)}, u32[]{:S(2)}) copy-start(bf16[1,352,2048]{2,1,0:T(8,128)(2,1)} %param.13) | copy-start | bytes 4325380
  92.5 22.6 %collective-permute-start.8 = (bf16[176,2048]{1,0:T(8,128)(2,1)}, bf16[176,2048]{1,0:T(8,128)(2,1)S(1)}, u32[]{:S(2)}, u32[]{:S(2)}) collective-permute-start(bf16[176,2048]{1,0:T(8,128)(2,1)} %add_convert_fusion), channel_id=1, source_target_pairs={{0,128},{64,192},{128,0},{192,64},{1,129},{65,193},{129,1},{193,65... | collective-permute-start | bytes 2162696 | tf_op jit(solution)/shard_map/ppermute | solution.py:280
  92.8 2.8 %copy-start.2 = (bf16[1,1,64,9,1408]{4,2,3,1,0:T(8,128)(2,1)S(1)}, bf16[1,1,64,9,1408]{4,2,3,1,0:T(8,128)(2,1)}, u32[]{:S(2)}) copy-start(bf16[1,1,64,9,1408]{4,2,3,1,0:T(8,128)(2,1)} %param.11) | copy-start | bytes 4866052
  92.8 2.8 %copy-start.4 = (bf16[1,1,64,9,1408]{4,2,3,1,0:T(8,128)(2,1)S(1)}, bf16[1,1,64,9,1408]{4,2,3,1,0:T(8,128)(2,1)}, u32[]{:S(2)}) copy-start(bf16[1,1,64,9,1408]{4,2,3,1,0:T(8,128)(2,1)} %param.12) | copy-start | bytes 4866052
  94.4 18.0 %copy-start.12 = (bf16[176,576]{1,0:T(8,128)(2,1)S(1)}, bf16[176,576]{1,0:T(8,128)(2,1)}, u32[]{:S(2)}) copy-start(bf16[176,576]{1,0:T(8,128)(2,1)} %copy-done.11) | copy-start | bytes 608260
  94.4 18.0 %copy-start.14 = (bf16[176,576]{1,0:T(8,128)(2,1)S(1)}, bf16[176,576]{1,0:T(8,128)(2,1)}, u32[]{:S(2)}) copy-start(bf16[176,576]{1,0:T(8,128)(2,1)} %copy-done.13) | copy-start | bytes 608260
  94.4 31.8 %collective-permute-start.6 = (bf16[176,2048]{1,0:T(8,128)(2,1)}, bf16[176,2048]{1,0:T(8,128)(2,1)}, u32[]{:S(2)}, u32[]{:S(2)}) collective-permute-start(bf16[176,2048]{1,0:T(8,128)(2,1)} %add_convert_fusion.1.refs_4_), channel_id=1, source_target_pairs={{0,128},{64,192},{128,0},{192,64},{1,129},{65,193},{129,1},{193,65... | collective-permute-start | bytes 2162696 | tf_op jit(solution)/shard_map/ppermute | solution.py:280
  104.9 23.4 %all-to-all-start.1 = ((f32[64,1,9]{2,1,0:T(1,128)}), f32[64,1,9]{2,1,0:T(1,128)}, u32[]{:S(2)}, u32[]{:S(2)}) async-start(f32[64,1,9]{2,1,0:T(1,128)} %bitcast.45), calls=%async_computation.1 | async-start | bytes 65536 | tf_op jit(solution)/shard_map/all_to_all | solution.py:297
  116.1 12.2 %copy-start.17 = (bf16[128,2]{0,1:T(2,128)(2,1)S(1)}, bf16[128,2]{0,1:T(2,128)(2,1)}, u32[]{:S(2)}) copy-start(bf16[128,2]{0,1:T(2,128)(2,1)} %param.10) | copy-start | bytes 1540
  (9 other events, 6.1 us)

commit v3 on v2

--- a/solution.py
+++ b/solution.py
@@ -78,7 +78,10 @@
         pltpu.make_async_copy(recv_ref.at[pl.ds(i * size, size), :], come.at[i], sems.at[i])
         for i in range(turns)
     ]
-    extra = [pltpu.make_async_copy(lefts[k], held.at[k], left_sems.at[k]) for k in range(cuts)]
+    part = lefts[0].shape[0]
+    extra = [
+        pltpu.make_async_copy(lefts[k], held.at[pl.ds(k * part, part), :], left_sems.at[k]) for k in range(cuts)
+    ]
     for load in loads + extra:
         load.start()
     blocks = scaled_ref.shape[1] // LANES
@@ -91,13 +94,16 @@
             scaled_ref[c * groups : (c + 1) * groups, j * LANES : (j + 1) * LANES] = wide[
                 pl.ds(c * blocks + j, groups, stride=span), :
             ].astype(BF16)
+    for load in extra:
+        load.wait()
+    whole = jnp.dot(held[...], scaled_ref[...], preferred_element_type=F32).astype(BF16)
     for k, out in enumerate(products):
-        extra[k].wait()
-        out[...] = jnp.dot(held[k], scaled_ref[...], preferred_element_type=F32).astype(BF16)
+        out[...] = whole[k * part : (k + 1) * part, :]
 
 
 def grads_kernel(cap, step, flips, me_ref, scaled_ref, gate_ref, up_ref, *refs):
-    gate_out, up_out, score_ref, token_ref, block_ref, gate_grad_ref, up_grad_ref, sems, out_sems = refs[-9:]
+    gate_out, up_out, score_ref, token_ref, block_ref, gate_grad_ref, up_grad_ref = refs[-12:-5]
+    act_ref, slope_ref, hidden_ref, sems, out_sems = refs[-5:]
     stores = []
     shares = refs[: len(flips)]
     part = shares[0].shape[0]
@@ -106,10 +112,19 @@
         place = pl.ds(pl.multiple_of((me_ref[0] ^ flip) * part, 16), part)
         loads.append(pltpu.make_async_copy(shares[at], block_ref.at[place, :], sems.at[at]))
         loads[-1].start()
+    token_ref[...] = jnp.zeros_like(token_ref)
+    width = block_ref.shape[0]
+    for at in range(0, width, LANES):
+        cols = slice(at, at + LANES)
+        gate = gate_ref[:, cols].astype(F32)
+        up = up_ref[:, cols].astype(F32)
+        sig = 1.0 / (1.0 + jnp.exp(-gate))
+        act = gate * sig
+        act_ref[:, cols] = act
+        slope_ref[:, cols] = up * (sig * (1.0 + gate * (1.0 - sig)))
+        hidden_ref[:, cols] = (act * up).astype(BF16)
     for load in loads:
         load.wait()
-    token_ref[...] = jnp.zeros_like(token_ref)
-    width = block_ref.shape[0]
     total = 0.0
     for lo in range(0, width, step):
         hi = min(lo + step, width)
@@ -119,14 +134,9 @@
         for at in range(lo, hi, LANES):
             cols = slice(at, at + LANES)
             grad = hidden_grad[:, at - lo : at - lo + LANES]
-            gate = gate_ref[:, cols].astype(F32)
-            up = up_ref[:, cols].astype(F32)
-            sig = 1.0 / (1.0 + jnp.exp(-gate))
-            act = gate * sig
-            up_grad = grad * act
-            total = total + grad * (act * up).astype(BF16).astype(F32)
-            gate_grad_ref[:, cols] = (grad * up * (sig * (1.0 + gate * (1.0 - sig)))).astype(BF16)
-            up_grad_ref[:, cols] = up_grad.astype(BF16)
+            total = total + grad * hidden_ref[:, cols].astype(F32)
+            gate_grad_ref[:, cols] = (grad * slope_ref[:, cols]).astype(BF16)
+            up_grad_ref[:, cols] = (grad * act_ref[:, cols]).astype(BF16)
         here = (slice(None), pl.ds(lo, hi - lo))
         for side, (held, out) in enumerate(((gate_grad_ref, gate_out), (up_grad_ref, up_out))):
             stores.append(pltpu.make_async_copy(held.at[here], out.at[here], out_sems.at[side, lo // step]))
@@ -257,7 +267,7 @@
         [
             pltpu.VMEM((total * blocks, LANES), F32),
             pltpu.VMEM((turns, total * blocks // turns, LANES), BF16),
-            pltpu.VMEM((cuts, size, total), BF16),
+            pltpu.VMEM((part, total), BF16),
             pltpu.SemaphoreType.DMA((turns,)),
             pltpu.SemaphoreType.DMA((cuts,)),
         ],
@@ -287,6 +297,9 @@
         [
             pltpu.VMEM((ff, width), BF16),
             pltpu.VMEM((total, ff), BF16),
+            pltpu.VMEM((total, ff), BF16),
+            pltpu.VMEM((total, ff), F32),
+            pltpu.VMEM((total, ff), F32),
             pltpu.VMEM((total, ff), BF16),
             pltpu.SemaphoreType.DMA((replicas,)),
             pltpu.SemaphoreType.DMA((2, -(-ff // (2 * LANES)))),

time: 131 us -> 130 us (level)
    pallas_call x8, Pallas kernels: 29.3 us -> 28 us  [call(): pl.pallas_call(kernel, grid=() if grid is None else (grid,), out_shape=[j...]
  transfers between devices with their start and end apart: 11 -> 11, of which waited for: 2 -> 2; matrix products, arithmetic and copies ran while one was open for 6% -> 6% of each run, Pallas kernels for 18% -> 17%
where the time goes in v3:
time: 130 us
  waiting for transfers between devices  55.6 us (43%)
  starting transfers between devices  30.9 us (24%)
  Pallas kernels  28 us (22%)
  matrix products  8.23 us (6%)
  local copies, waits for them, and re-layouts  6.14 us (5%)
    all_to_all x1, waiting for transfers between devices, local(): lax.all_to_all(send.reshape(groups, cap * blocks, LANES), 'expert', split...  44.4 us
    pallas_call x8, Pallas kernels, call(): pl.pallas_call(kernel, grid=() if grid is None else (grid,), out_shape=[j...  28 us
    all_to_all x1, starting transfers between devices, local(): lax.all_to_all(send.reshape(groups, cap * blocks, LANES), 'expert', split...  15.6 us
    ppermute x2, waiting for transfers between devices, local(): crossed = [lax.ppermute(x, 'dp', over_chip) for x in far]  11.2 us
    dot_general x4, matrix products, product(): return jnp.dot(left, scaled, preferred_element_type=F32)  8.23 us
    all_to_all x1, starting transfers between devices, local(): lax.all_to_all(score.reshape(groups, 1, cap), 'expert', split_axis=0, con...  7.44 us
    unnamed x44, local copies, waits for them, and re-layouts  6.14 us
    ppermute x4, starting transfers between devices, to_core(): return lax.ppermute(x.astype(BF16), 'dp', over_core)  4.28 us
  transfers between devices with their start and end apart: 11, of which 2 were waited for; matrix products, arithmetic and copies ran while one was open for 6% of the time, Pallas kernels for 17%

profile of v3, /device:TPU:1, one launch (start us, length us, event | category | flops | bytes accessed | tf_op | source)
XLA Modules:
  0.0 129.7 jit_solution(14164505959680244717)
XLA Ops:
  0.6 4.5 %shard_map.102 = (bf16[9216,128]{1,0:T(8,128)(2,1)}, s32[2,128]{1,0:T(2,128)}) custom-call(s32[2,128]{1,0:T(2,128)} %bitcast.54, s32[2,128]{1,0:T(2,128)} %bitcast.55, bf16[2,128]{1,0:T(2,128)(2,1)} %bitcast.46, bf16[128,2048]{1,0:T(8,128)(2,1)} %grad_ref.1), custom_call_target="tpu_custom_call" | custom-call | flops 301989888 | bytes 7077888 | tf_op jit(solution)/shard_map/pallas_call | solution.py:194
  5.2 15.6 %all-to-all-start = ((bf16[64,144,128]{2,1,0:T(8,128)(2,1)}), bf16[64,144,128]{2,1,0:T(8,128)(2,1)}, u32[]{:S(2)}, u32[]{:S(2)}) async-start(bf16[64,144,128]{2,1,0:T(8,128)(2,1)} %bitcast.52), calls=%async_computation | async-start | bytes 4718592 | tf_op jit(solution)/shard_map/all_to_all | solution.py:240
  21.2 1.2 collective-permute-start.3
  22.4 2.8 %shard_map.103 = (bf16[176,576]{1,0:T(8,128)(2,1)S(1)}, bf16[176,576]{1,0:T(8,128)(2,1)S(1)}, bf16[176,576]{1,0:T(8,128)(2,1)S(1)}, bf16[176,576]{1,0:T(8,128)(2...) custom-call(s32[1]{0:T(128)} %bitcast.5.me_ref, ...), custom_call_target="tpu_custom_call" | custom-call | flops 16220160 | bytes 6488064 | tf_op jit(solution)/shard_map/pallas_call | solution.py:194
  25.9 0.7 copy-done.7
  26.6 0.7 copy-done.9
  27.3 0.7 copy-done.11
  28.0 0.7 copy-done.13
  29.4 0.7 copy-done.20
  30.7 44.4 %all-to-all-done = bf16[64,144,128]{2,1,0:T(8,128)(2,1)} async-done(((bf16[64,144,128]{2,1,0:T(8,128)(2,1)}), bf16[64,144,128]{2,1,0:T(8,128)(2,1)}, u32[]{:S(2)}, u32[]{:S(2)}) %all-to-all-start) | async-done | bytes 2359328 | tf_op jit(solution)/shard_map/all_to_all | solution.py:240
  75.1 5.7 %shard_map.104 = (bf16[576,2048]{1,0:T(8,128)(2,1)}, bf16[176,2048]{1,0:T(8,128)(2,1)}, bf16[176,2048]{1,0:T(8,128)(2,1)}) custom-call(bf16[9216,128]{1,0:T(8,128)(2,1)} %bitcast.4.recv_ref, bf16[176,576]{1,0:T(8,128)(2,1)} %copy-done.19, bf16[176,576]{1,0:T(8,128)(2,1)} %copy-done.20, f32[8,128]{1,0:T(8,128)} %copy-done.21), custom_call_target="tpu_custom_call" | custom-call | flops 830472192 | bytes 9437184 | tf_op jit(solution)/shard_map/pallas_call | solution.py:194
  80.8 3.7 %collective-permute-start.7 = (bf16[176,2048]{1,0:T(8,128)(2,1)}, bf16[176,2048]{1,0:T(8,128)(2,1)S(1)}, u32[]{:S(2)}, u32[]{:S(2)}) collective-permute-start(bf16[176,2048]{1,0:T(8,128)(2,1)} %get-tuple-element.33), channel_id=1, source_target_pairs={{0,64},{64,0},{128,192},{192,128},{1,65},{65,1},{129,193},{193,129... | collective-permute-start | bytes 2162696 | tf_op jit(solution)/shard_map/ppermute | solution.py:283
  85.0 3.4 %convolution_convert_fusion = bf16[176,2048]{1,0:T(8,128)(2,1)} fusion(bf16[176,576]{1,0:T(8,128)(2,1)S(1)} %copy-done.10, bf16[576,2048]{1,0:T(8,128)(2,1)} %get-tuple-element.28.scaled_ref), kind=kOutput, calls=%fused_computation | convolution fusion | flops 415596544 | bytes 3282944 | tf_op jit(solution)/shard_map/dot_general | solution.py:280
  88.5 1.6 %convolution_convert_fusion.1 = bf16[176,2048]{1,0:T(8,128)(2,1)} fusion(bf16[176,576]{1,0:T(8,128)(2,1)S(1)} %copy-done.8, bf16[576,2048]{1,0:T(8,128)(2,1)S(1)} %copy-done), kind=kOutput, calls=%fused_computation.1 | convolution fusion | flops 415596544 | bytes 3282944 | tf_op jit(solution)/shard_map/dot_general | solution.py:280
  90.6 1.6 %add_convert_fusion = bf16[176,2048]{1,0:T(8,128)(2,1)} fusion(bf16[176,2048]{1,0:T(8,128)(2,1)S(1)} %collective-permute-done.7, bf16[176,576]{1,0:T(8,128)(2,1)S(1)} %copy-done.6, bf16[576,2048]{1,0:T(8,128)(2,1)S(1)} %copy-done), kind=kOutput, calls=%fused_computation.2 | convolution fusion | flops 416317440 | bytes 4003840 | tf_op jit(solution)/shard_map/dot_general | solution.py:280
  92.5 1.6 %add_convert_fusion.1.refs_4_ = bf16[176,2048]{1,0:T(8,128)(2,1)} fusion(bf16[176,2048]{1,0:T(8,128)(2,1)S(1)} %collective-permute-done.5, bf16[176,576]{1,0:T(8,128)(2,1)S(1)} %get-tuple-element.35, bf16[576,2048]{1,0:T(8,128)(2,1)S(1)} %copy-done), kind=kOutput, calls=%fused_computation.3 | convolution fusion | flops 416317440 | bytes 4003840 | tf_op jit(solution)/shard_map/dot_general | solution.py:280
  94.1 1.2 collective-permute-start.6
  95.3 7.6 %shard_map.105 = (bf16[576,1408]{1,0:T(8,128)(2,1)}, bf16[576,1408]{1,0:T(8,128)(2,1)}, f32[64,9]{1,0:T(8,128)S(1)}, f32[8,128]{1,0:T(8,128)S(1)}) custom-call(s32[1]{0:T(128)} %bitcast.5.me_ref, bf16[576,2048]{1,0:T(8,128)(2,1)S(1)} %copy-done, bf16[576,1408]{1,0:T(8,128)(2,1)S(1)} %bitcast.42, bf16[576,1408]{1,0:T(8,128)(2,1)S(1)} %bitcast.44, ...), custom_call_target="tpu_custom_call" | custom-call | flops 3321888768 | bytes 14614528 | tf_op jit(solution)/shard_map/pallas_call | solution.py:194
  103.5 7.4 %all-to-all-start.1 = ((f32[64,1,9]{2,1,0:T(1,128)}), f32[64,1,9]{2,1,0:T(1,128)}, u32[]{:S(2)}, u32[]{:S(2)}) async-start(f32[64,1,9]{2,1,0:T(1,128)} %bitcast.45), calls=%async_computation.1 | async-start | bytes 65536 | tf_op jit(solution)/shard_map/all_to_all | solution.py:310
  111.0 2.6 %shard_map.106.near_ref = f32[352,2048]{1,0:T(8,128)S(1)} custom-call(bf16[576,2048]{1,0:T(8,128)(2,1)S(1)} %copy-done, bf16[176,576]{1,0:T(8,128)(2,1)S(1)} %copy-done.12, bf16[176,576]{1,0:T(8,128)(2,1)S(1)} %copy-done.14, bf16[176,2048]{1,0:T(8,128)(2,1)} %collective-permute-done.refs_2_, bf16[176,2048]{1,0:T(8,128)(2,1)} %collective-permute-done.1.refs_3_, ...), custom_call_target="tpu_custom_call" | custom-call | flops 830472192 | bytes 5767168 | tf_op jit(solution)/shard_map/pallas_call | solution.py:194
  113.7 1.0 shard_map.107.refs_0_
  114.7 11.2 %collective-permute-done.6.far_ref = bf16[176,2048]{1,0:T(8,128)(2,1)} collective-permute-done((bf16[176,2048]{1,0:T(8,128)(2,1)}, bf16[176,2048]{1,0:T(8,128)(2,1)}, u32[]{:S(2)}, u32[]{:S(2)}) %collective-permute-start.6) | collective-permute-done | bytes 720928 | tf_op jit(solution)/shard_map/ppermute | solution.py:290
  125.9 2.1 %shard_map.108 = bf16[352,2048]{1,0:T(8,128)(2,1)} custom-call(f32[352,2048]{1,0:T(8,128)S(1)} %shard_map.106.near_ref, bf16[176,2048]{1,0:T(8,128)(2,1)} %collective-permute-done.6.far_ref, bf16[352,2048]{1,0:T(8,128)(2,1)} %shard_map.107.refs_0_), custom_call_target="tpu_custom_call", output_to_operand_aliasing={{}: (2, {})} | custom-call | flops 360448 | bytes 2883584 | tf_op jit(solution)/shard_map/pallas_call | solution.py:194
  128.1 1.6 %shard_map.109 = f32[2,128]{1,0:T(2,128)} custom-call(f32[64,9]{1,0:T(8,128)} %bitcast.26.back_ref, s32[2,128]{1,0:T(2,128)S(1)} %copy-done.16, bf16[2,128]{1,0:T(2,128)(2,1)S(1)} %bitcast.47, f32[8,128]{1,0:T(8,128)S(1)} %get-tuple-element.37.refs_4_.refs_0_), custom_call_target="tpu_custom_call" | custom-call | flops 73728 | bytes 294912 | tf_op jit(solution)/shard_map/pallas_call | solution.py:194
  (54 shorter events, 4.4 us)
Async XLA Ops:
  5.1 17.3 %copy-start.1 = (bf16[1,1,64,9,1408]{4,2,3,1,0:T(8,128)(2,1)S(1)}, bf16[1,1,64,9,1408]{4,2,3,1,0:T(8,128)(2,1)}, u32[]{:S(2)}) copy-start(bf16[1,1,64,9,1408]{4,2,3,1,0:T(8,128)(2,1)} %param.11) | copy-start | bytes 4866052
  5.1 17.3 %copy-start.3 = (bf16[1,1,64,9,1408]{4,2,3,1,0:T(8,128)(2,1)S(1)}, bf16[1,1,64,9,1408]{4,2,3,1,0:T(8,128)(2,1)}, u32[]{:S(2)}) copy-start(bf16[1,1,64,9,1408]{4,2,3,1,0:T(8,128)(2,1)} %param.12) | copy-start | bytes 4866052
  5.1 17.3 %copy-start.16 = (s32[2,128]{1,0:T(2,128)S(1)}, s32[2,128]{1,0:T(2,128)}, u32[]{:S(2)}) copy-start(s32[2,128]{1,0:T(2,128)} %get-tuple-element.24.after_ref.dest_ref) | copy-start | bytes 3076
  5.2 70.0 %all-to-all-start = ((bf16[64,144,128]{2,1,0:T(8,128)(2,1)}), bf16[64,144,128]{2,1,0:T(8,128)(2,1)}, u32[]{:S(2)}, u32[]{:S(2)}) async-start(bf16[64,144,128]{2,1,0:T(8,128)(2,1)} %bitcast.52), calls=%async_computation | async-start | bytes 4718592 | tf_op jit(solution)/shard_map/all_to_all | solution.py:240
  20.8 63.8 %collective-permute-start.2 = (bf16[352,2048]{1,0:T(8,128)(2,1)}, bf16[352,2048]{1,0:T(8,128)(2,1)}, u32[]{:S(2)}, u32[]{:S(2)}) collective-permute-start(bf16[352,2048]{1,0:T(8,128)(2,1)} %bitcast.48), channel_id=1, source_target_pairs={{0,128},{64,192},{128,0},{192,64},{1,129},{65,193},{129,1},{193,65... | collective-permute-start | bytes 4325384 | tf_op jit(solution)/shard_map/ppermute | solution.py:222
  21.2 72.9 %collective-permute-start.3 = (bf16[352,2048]{1,0:T(8,128)(2,1)}, bf16[352,2048]{1,0:T(8,128)(2,1)}, u32[]{:S(2)}, u32[]{:S(2)}) collective-permute-start(bf16[352,2048]{1,0:T(8,128)(2,1)} %bitcast.49), channel_id=1, source_target_pairs={{0,64},{64,0},{128,192},{192,128},{1,65},{65,1},{129,193},{193,129... | collective-permute-start | bytes 4325384 | tf_op jit(solution)/shard_map/ppermute | solution.py:223
  75.1 9.9 %copy-start.10 = (bf16[176,576]{1,0:T(8,128)(2,1)S(1)}, bf16[176,576]{1,0:T(8,128)(2,1)}, u32[]{:S(2)}) copy-start(bf16[176,576]{1,0:T(8,128)(2,1)} %copy-done.9) | copy-start | bytes 608260
  80.8 9.3 %collective-permute-start.7 = (bf16[176,2048]{1,0:T(8,128)(2,1)}, bf16[176,2048]{1,0:T(8,128)(2,1)S(1)}, u32[]{:S(2)}, u32[]{:S(2)}) collective-permute-start(bf16[176,2048]{1,0:T(8,128)(2,1)} %get-tuple-element.33), channel_id=1, source_target_pairs={{0,64},{64,0},{128,192},{192,128},{1,65},{65,1},{129,193},{193,129... | collective-permute-start | bytes 2162696 | tf_op jit(solution)/shard_map/ppermute | solution.py:283
  84.5 7.7 %collective-permute-start.5 = (bf16[176,2048]{1,0:T(8,128)(2,1)}, bf16[176,2048]{1,0:T(8,128)(2,1)S(1)}, u32[]{:S(2)}, u32[]{:S(2)}) collective-permute-start(bf16[176,2048]{1,0:T(8,128)(2,1)} %get-tuple-element.36), channel_id=1, source_target_pairs={{0,64},{64,0},{128,192},{192,128},{1,65},{65,1},{129,193},{193,129... | collective-permute-start | bytes 2162696 | tf_op jit(solution)/shard_map/ppermute | solution.py:283
  84.6 10.7 %collective-permute-start.4 = (bf16[352,2048]{1,0:T(8,128)(2,1)}, bf16[352,2048]{1,0:T(8,128)(2,1)S(1)}, u32[]{:S(2)}, u32[]{:S(2)}) collective-permute-start(bf16[352,2048]{1,0:T(8,128)(2,1)} %collective-permute-done.2.refs_1_), channel_id=1, source_target_pairs={{0,64},{64,0},{128,192},{192,128},{1,65},{65,1},{129,193},{193,129... | collective-permute-start | bytes 4325384 | tf_op jit(solution)/shard_map/ppermute | solution.py:287
  85.0 3.5 %copy-start = (bf16[576,2048]{1,0:T(8,128)(2,1)S(1)}, bf16[576,2048]{1,0:T(8,128)(2,1)}, u32[]{:S(2)}) copy-start(bf16[576,2048]{1,0:T(8,128)(2,1)} %get-tuple-element.28.scaled_ref) | copy-start | bytes 7077892
  85.0 3.5 %copy-start.8 = (bf16[176,576]{1,0:T(8,128)(2,1)S(1)}, bf16[176,576]{1,0:T(8,128)(2,1)}, u32[]{:S(2)}) copy-start(bf16[176,576]{1,0:T(8,128)(2,1)} %copy-done.7) | copy-start | bytes 608260
  88.4 22.6 %collective-permute-start.1 = (bf16[176,2048]{1,0:T(8,128)(2,1)}, bf16[176,2048]{1,0:T(8,128)(2,1)}, u32[]{:S(2)}, u32[]{:S(2)}) collective-permute-start(bf16[176,2048]{1,0:T(8,128)(2,1)} %convolution_convert_fusion), channel_id=1, source_target_pairs={{0,64},{64,0},{128,192},{192,128},{1,65},{65,1},{129,193},{193,129... | collective-permute-start | bytes 2162696 | tf_op jit(solution)/shard_map/ppermute | solution.py:283
  88.5 2.0 %copy-start.6 = (bf16[176,576]{1,0:T(8,128)(2,1)S(1)}, bf16[176,576]{1,0:T(8,128)(2,1)}, u32[]{:S(2)}) copy-start(bf16[176,576]{1,0:T(8,128)(2,1)} %copy-done.5) | copy-start | bytes 608260
  90.2 20.8 %collective-permute-start = (bf16[176,2048]{1,0:T(8,128)(2,1)}, bf16[176,2048]{1,0:T(8,128)(2,1)}, u32[]{:S(2)}, u32[]{:S(2)}) collective-permute-start(bf16[176,2048]{1,0:T(8,128)(2,1)} %convolution_convert_fusion.1), channel_id=1, source_target_pairs={{0,64},{64,0},{128,192},{192,128},{1,65},{65,1},{129,193},{193,129... | collective-permute-start | bytes 2162696 | tf_op jit(solution)/shard_map/ppermute | solution.py:283
  90.6 4.7 %copy-start.18 = (bf16[1,352,2048]{2,1,0:T(8,128)(2,1)S(1)}, bf16[1,352,2048]{2,1,0:T(8,128)(2,1)}, u32[]{:S(2)}) copy-start(bf16[1,352,2048]{2,1,0:T(8,128)(2,1)} %param.13) | copy-start | bytes 4325380
  92.2 21.5 %collective-permute-start.8 = (bf16[176,2048]{1,0:T(8,128)(2,1)}, bf16[176,2048]{1,0:T(8,128)(2,1)S(1)}, u32[]{:S(2)}, u32[]{:S(2)}) collective-permute-start(bf16[176,2048]{1,0:T(8,128)(2,1)} %add_convert_fusion), channel_id=1, source_target_pairs={{0,128},{64,192},{128,0},{192,64},{1,129},{65,193},{129,1},{193,65... | collective-permute-start | bytes 2162696 | tf_op jit(solution)/shard_map/ppermute | solution.py:290
  92.5 2.8 %copy-start.2 = (bf16[1,1,64,9,1408]{4,2,3,1,0:T(8,128)(2,1)S(1)}, bf16[1,1,64,9,1408]{4,2,3,1,0:T(8,128)(2,1)}, u32[]{:S(2)}) copy-start(bf16[1,1,64,9,1408]{4,2,3,1,0:T(8,128)(2,1)} %param.11) | copy-start | bytes 4866052
  92.5 2.8 %copy-start.4 = (bf16[1,1,64,9,1408]{4,2,3,1,0:T(8,128)(2,1)S(1)}, bf16[1,1,64,9,1408]{4,2,3,1,0:T(8,128)(2,1)}, u32[]{:S(2)}) copy-start(bf16[1,1,64,9,1408]{4,2,3,1,0:T(8,128)(2,1)} %param.12) | copy-start | bytes 4866052
  94.1 16.9 %copy-start.12 = (bf16[176,576]{1,0:T(8,128)(2,1)S(1)}, bf16[176,576]{1,0:T(8,128)(2,1)}, u32[]{:S(2)}) copy-start(bf16[176,576]{1,0:T(8,128)(2,1)} %copy-done.11) | copy-start | bytes 608260
  94.1 16.9 %copy-start.14 = (bf16[176,576]{1,0:T(8,128)(2,1)S(1)}, bf16[176,576]{1,0:T(8,128)(2,1)}, u32[]{:S(2)}) copy-start(bf16[176,576]{1,0:T(8,128)(2,1)} %copy-done.13) | copy-start | bytes 608260
  94.1 31.8 %collective-permute-start.6 = (bf16[176,2048]{1,0:T(8,128)(2,1)}, bf16[176,2048]{1,0:T(8,128)(2,1)}, u32[]{:S(2)}, u32[]{:S(2)}) collective-permute-start(bf16[176,2048]{1,0:T(8,128)(2,1)} %add_convert_fusion.1.refs_4_), channel_id=1, source_target_pairs={{0,128},{64,192},{128,0},{192,64},{1,129},{65,193},{129,1},{193,65... | collective-permute-start | bytes 2162696 | tf_op jit(solution)/shard_map/ppermute | solution.py:290
  103.5 24.5 %all-to-all-start.1 = ((f32[64,1,9]{2,1,0:T(1,128)}), f32[64,1,9]{2,1,0:T(1,128)}, u32[]{:S(2)}, u32[]{:S(2)}) async-start(f32[64,1,9]{2,1,0:T(1,128)} %bitcast.45), calls=%async_computation.1 | async-start | bytes 65536 | tf_op jit(solution)/shard_map/all_to_all | solution.py:310
  114.7 13.3 %copy-start.17 = (bf16[128,2]{0,1:T(2,128)(2,1)S(1)}, bf16[128,2]{0,1:T(2,128)(2,1)}, u32[]{:S(2)}) copy-start(bf16[128,2]{0,1:T(2,128)(2,1)} %param.10) | copy-start | bytes 1540
  (9 other events, 6.1 us)
